TPU v7x, 256 devices: a whole 4x4x8 slice. The times are simulated.
256 devices in a mesh: len: 4 (over y_hi, core), eng: 64 (over z, y_lo, x).
Axes of the slice: x: 4, y: 4 (y_hi: 2, y_lo: 2; y = y_hi * 2 + y_lo), z: 8, core: 2. Of those that a mesh axis runs over, the one named last changes fastest.
Arguments:
- less_green: bfloat16 [4, 2048, 2, 128, 128], P('len', 'eng'), may hold values from -6 to 6
- greater_green: bfloat16 [4, 2048, 2, 128, 128], P('len', 'eng'), may hold values from -6 to 6
- coulomb: bfloat16 [4, 2, 128, 128], P('len'), may hold values from -0.3125 to 0.3125
Outputs:
- polarization: bfloat16 [4, 2048, 2, 128, 128], P('len', 'eng')
- screened: bfloat16 [4, 2048, 4, 128, 128], P('len', 'eng')
All inputs are finite; a program needn't handle non-finite values.
Results may differ from a plain program's by a relative error of at most 0.0057.
Values may be sent and summed in bfloat16 or wider, within the bound.
No kernel may reach another device: no remote copies, remote signals or barrier semaphores. Data moves between devices by JAX's collectives and lax.ppermute only.
A program may use at most 128 MiB of HBM per device.

v0:
```python
import math

import jax
import jax.numpy as jnp
from jax import lax
from jax.sharding import PartitionSpec as P

radix_size = 64


def with_halo(cells, sides, width):
    for axis, dim in sides:
        count = lax.axis_size(axis)
        ends = count - 1
        head = lax.slice_in_dim(cells, 0, width, axis=dim)
        tail = lax.slice_in_dim(cells, cells.shape[dim] - width, cells.shape[dim], axis=dim)
        cells = jnp.concatenate(
            [
                lax.ppermute(tail, axis, [(i, (i + 1) % count) for i in range(ends)]),
                cells,
                lax.ppermute(head, axis, [((i + 1) % count, i) for i in range(ends)]),
            ],
            axis=dim,
        )
    return cells


def unit_table(row_total, col_total, period, direction):
    product = (
        jnp.arange(row_total, dtype=jnp.int32)[:, None]
        * jnp.arange(col_total, dtype=jnp.int32)[None, :]
        % period
    )
    angles = product.astype(jnp.float32) * (direction * 2.0 * math.pi / period)
    return (jnp.cos(angles), jnp.sin(angles))


def complex_mix(pattern, left_pair, right_pair):
    highest = lax.Precision.HIGHEST
    real_part = jnp.einsum(pattern, left_pair[0], right_pair[0], precision=highest) - jnp.einsum(
        pattern, left_pair[1], right_pair[1], precision=highest
    )
    imag_part = jnp.einsum(pattern, left_pair[0], right_pair[1], precision=highest) + jnp.einsum(
        pattern, left_pair[1], right_pair[0], precision=highest
    )
    return (real_part, imag_part)


def twist(pair, table):
    cos_part = table[0][:, :, None]
    sin_part = table[1][:, :, None]
    return (pair[0] * cos_part - pair[1] * sin_part, pair[0] * sin_part + pair[1] * cos_part)


def forward(values, energies):
    period = 2 * energies
    inner_len = period // radix_size
    half_radix = radix_size // 2
    first_tab = unit_table(radix_size, half_radix, radix_size, -1.0)
    twiddle = unit_table(radix_size, inner_len, period, -1.0)
    second_tab = unit_table(inner_len, inner_len, inner_len, -1.0)
    shaped = (
        values[0].reshape(half_radix, inner_len, -1),
        values[1].reshape(half_radix, inner_len, -1),
    )
    sectioned = twist(complex_mix("kn,nms->kms", first_tab, shaped), twiddle)
    return complex_mix("qm,kms->kqs", second_tab, sectioned)


def inverse(spectrum, energies):
    period = 2 * energies
    inner_len = period // radix_size
    half_radix = radix_size // 2
    first_back = unit_table(half_radix, radix_size, radix_size, 1.0)
    twiddle_back = unit_table(radix_size, inner_len, period, 1.0)
    second_back = unit_table(inner_len, inner_len, inner_len, 1.0)
    sectioned = twist(complex_mix("mq,kqs->kms", second_back, spectrum), twiddle_back)
    result_pair = complex_mix("nk,kms->nms", first_back, sectioned)
    return (
        result_pair[0].reshape(energies, -1) / period,
        result_pair[1].reshape(energies, -1) / period,
    )


def correlate(pieces):
    less_piece, greater_piece = pieces
    row_count, energies, parts, row_span, col_span = less_piece.shape

    def series(values):
        flattened = (
            jnp.transpose(values, (1, 2, 0, 3, 4))
            .reshape(energies, parts, row_count * row_span * col_span)
            .astype(jnp.float32)
        )
        return (flattened[:, 0], flattened[:, 1])

    less_spec = forward(series(less_piece), energies)
    greater_spec = forward(series(greater_piece), energies)
    prod_re = less_spec[0] * greater_spec[0] + less_spec[1] * greater_spec[1]
    prod_im = less_spec[1] * greater_spec[0] - less_spec[0] * greater_spec[1]
    summed = inverse((prod_re, prod_im), energies)
    factor = 1.0 / math.sqrt(energies)
    polar = jnp.stack((-summed[1] * factor, summed[0] * factor), axis=1).astype(jnp.bfloat16)
    return jnp.transpose(
        polar.reshape(energies, parts, row_count, row_span, col_span), (2, 0, 1, 3, 4)
    )


def spectrum_step(pieces):
    polar = correlate(pieces)
    return polar


def left_apply(matrix, fields, flipped):
    pattern = "rji,recjk->recik" if flipped else "rij,recjk->recik"
    return jnp.einsum(pattern, matrix, fields, preferred_element_type=jnp.float32).astype(
        jnp.bfloat16
    )


def right_apply(fields, matrix, flipped):
    pattern = "recij,rkj->recik" if flipped else "recij,rjk->recik"
    return jnp.einsum(pattern, fields, matrix, preferred_element_type=jnp.float32)


def body(less_green, greater_green, coulomb):
    polar = spectrum_step(
        (
            lax.all_to_all(less_green, "eng", split_axis=3, concat_axis=1, tiled=True),
            lax.all_to_all(greater_green, "eng", split_axis=3, concat_axis=1, tiled=True),
        )
    )
    polar = lax.all_to_all(polar, "eng", split_axis=1, concat_axis=3, tiled=True)
    padded = with_halo(polar, (("len", 0),), 1)
    framed = with_halo(coulomb, (("len", 0),), 1)
    own_diag = framed[1:-1, 0]
    own_up = framed[1:-1, 1]
    prev_up = framed[:-2, 1]
    next_diag = framed[2:, 0]
    from_lower = left_apply(prev_up, padded[:-2], True)
    from_own = left_apply(own_diag, padded[1:-1], False)
    from_upper = left_apply(own_up, padded[2:], False)
    diag_block = (
        right_apply(from_lower, prev_up, False)
        + right_apply(from_own, own_diag, False)
        + right_apply(from_upper, own_up, True)
    )
    upper_block = right_apply(from_own, own_up, False) + right_apply(from_upper, next_diag, False)
    screened = jnp.concatenate((diag_block, upper_block), axis=2).astype(jnp.bfloat16)
    return (polar, screened)


def solution(mesh):
    in_specs = (
        P("len", "eng", None, None, None),
        P("len", "eng", None, None, None),
        P("len", None, None, None),
    )
    out_specs = (P("len", "eng", None, None, None), P("len", "eng", None, None, None))
    return jax.shard_map(body, mesh=mesh, in_specs=in_specs, out_specs=out_specs, check_vma=False)
```

profile of v0, /device:TPU:1, one launch (start us, length us, event | category | flops | bytes accessed | tf_op | source)
XLA Modules:
  0.0 384.3 jit_solution(8836655379173896203)
XLA Ops:
  4.9 13.5 %all-to-all-start = ((bf16[1,32,2,128,128]{4,1,2,0,3:T(8,128)(2,1)}), bf16[1,32,2,128,128]{4,1,2,0,3:T(8,128)(2,1)S(1)}, u32[]{:S(2)}, u32[]{:S(2)}) async-start(bf16[1,32,2,128,128]{4,1,2,0,3:T(8,128)(2,1)} %copy.104), calls=%async_computation | async-start | bytes 4194304 | tf_op jit(solution)/shard_map/all_to_all | solution.py:129
  22.7 44.2 %all-to-all-done = bf16[1,32,2,128,128]{4,1,2,0,3:T(8,128)(2,1)S(1)} async-done(((bf16[1,32,2,128,128]{4,1,2,0,3:T(8,128)(2,1)}), bf16[1,32,2,128,128]{4,1,2,0,3:T(8,128)(2,1)S(1)}, u32[]{:S(2)}, u32[]{:S(2)}) %all-to-all-start) | async-done | bytes 2097184 | tf_op jit(solution)/shard_map/all_to_all | solution.py:129
  66.8 8.1 %all-to-all-start.1 = ((bf16[1,32,2,128,128]{4,1,2,0,3:T(8,128)(2,1)}), bf16[1,32,2,128,128]{4,1,2,0,3:T(8,128)(2,1)}, u32[]{:S(2)}, u32[]{:S(2)}) async-start(bf16[1,32,2,128,128]{4,1,2,0,3:T(8,128)(2,1)} %copy.114), calls=%async_computation.1 | async-start | bytes 4194304 | tf_op jit(solution)/shard_map/all_to_all | solution.py:130
  86.2 35.6 %all-to-all-done.1 = bf16[1,32,2,128,128]{4,1,2,0,3:T(8,128)(2,1)} async-done(((bf16[1,32,2,128,128]{4,1,2,0,3:T(8,128)(2,1)}), bf16[1,32,2,128,128]{4,1,2,0,3:T(8,128)(2,1)}, u32[]{:S(2)}, u32[]{:S(2)}) %all-to-all-start.1) | async-done | bytes 2097184 | tf_op jit(solution)/shard_map/all_to_all | solution.py:130
  121.7 6.1 %copy.216 = bf16[1,32,2,64,2,128]{5,4,1,3,2,0:T(2,128)(2,1)} copy(bf16[1,32,2,64,2,128]{5,1,2,4,3,0:T(8,128)(2,1)} %bitcast.9) | data formatting | bytes 4194304 | tf_op jit(solution)/shard_map/all_to_all | solution.py:130
  156.9 8.7 %multiply_subtract_fusion.1 = (f32[64,64,256]{2,0,1:T(8,128)S(1)}, f32[64,64,256]{2,0,1:T(8,128)S(1)}, f32[64,64,256]{2,0,1:T(8,128)S(1)}, f32[64,64,256]{2,0,1:T(8,128)S(1)}) fusion(f32[64,64,256]{2,0,1:T(8,128)} %convolution_subtract_fusion, f32[64,64]{0,1:T(8,128)S(1)} %copy.111, f32[64,64]{0,1:T(8,128)S(1)} %copy.108, ...), kind=kOutput, calls=%fused_computation.16 | convolution fusion | flops 416313344 | bytes 34635776 | tf_op jit(solution)/shard_map/kn,nms->kms/dot_general | solution.py:43
  165.6 6.4 %fusion.16 = f32[64,256,64]{1,2,0:T(8,128)S(1)} fusion(f32[64,64,256]{2,0,1:T(8,128)S(1)} %get-tuple-element.15), kind=kOutput, calls=%fused_computation.27 | convolution fusion | flops 805363712 | bytes 8388608 | tf_op jit(solution)/shard_map/qm,kms->kqs/dot_general | solution.py:43
  172.1 6.7 %fusion.18 = f32[64,256,64]{1,2,0:T(8,128)S(1)} fusion(f32[64,64,256]{2,0,1:T(8,128)S(1)} %get-tuple-element.15), kind=kOutput, calls=%fused_computation.29 | convolution fusion | flops 805363712 | bytes 8388608 | tf_op jit(solution)/shard_map/qm,kms->kqs/dot_general | solution.py:40
  178.7 7.2 %fusion.24 = f32[64,256,64]{1,2,0:T(8,128)} fusion(f32[64,64,256]{2,0,1:T(8,128)S(1)} %get-tuple-element.22), kind=kOutput, calls=%fused_computation.35 | convolution fusion | flops 805363712 | bytes 8388608 | tf_op jit(solution)/shard_map/qm,kms->kqs/dot_general | solution.py:43
  185.9 6.5 %fusion.26 = f32[64,256,64]{1,2,0:T(8,128)S(1)} fusion(f32[64,64,256]{2,0,1:T(8,128)S(1)} %get-tuple-element.22), kind=kOutput, calls=%fused_computation.37 | convolution fusion | flops 805363712 | bytes 8388608 | tf_op jit(solution)/shard_map/qm,kms->kqs/dot_general | solution.py:40
  192.4 7.3 %fusion.38 = f32[64,256,64]{1,2,0:T(8,128)S(1)} fusion(f32[64,256,64]{1,2,0:T(8,128)S(1)} %fusion.18, f32[64,64,256]{2,0,1:T(8,128)S(1)} %get-tuple-element.14), kind=kOutput, calls=%fused_computation.45 | convolution fusion | flops 806412288 | bytes 12582912 | tf_op jit(solution)/shard_map/qm,kms->kqs/dot_general | solution.py:40
  199.8 7.2 %fusion.41 = f32[64,256,64]{1,2,0:T(8,128)} fusion(f32[64,256,64]{1,2,0:T(8,128)S(1)} %fusion.16, f32[64,64,256]{2,0,1:T(8,128)S(1)} %get-tuple-element.14), kind=kOutput, calls=%fused_computation.46 | convolution fusion | flops 806412288 | bytes 12582912 | tf_op jit(solution)/shard_map/qm,kms->kqs/dot_general | solution.py:43
  207.0 7.3 %fusion.32 = f32[64,256,64]{1,2,0:T(8,128)} fusion(f32[64,256,64]{1,2,0:T(8,128)S(1)} %fusion.26, f32[64,64,256]{2,0,1:T(8,128)S(1)} %get-tuple-element.23), kind=kOutput, calls=%fused_computation.43 | convolution fusion | flops 806412288 | bytes 12582912 | tf_op jit(solution)/shard_map/qm,kms->kqs/dot_general | solution.py:40
  214.3 10.4 %multiply_add_fusion = (f32[64,256,64]{1,2,0:T(8,128)S(1)}, f32[64,256,64]{1,2,0:T(8,128)S(1)}) fusion(f32[64,256,64]{1,2,0:T(8,128)} %fusion.41, f32[64,256,64]{1,2,0:T(8,128)} %fusion.32, f32[64,256,64]{1,2,0:T(8,128)S(1)} %fusion.38, f32[64,256,64]{1,2,0:T(8,128)} %fusion.24, f32[64,64,256]{2,0,1:T(8,128)S(1)} %get-tuple-element.23), kind=kOutput, calls=%fused_computation.14 | convolution fusion | flops 812703744 | bytes 29360128 | tf_op jit(solution)/shard_map/qm,kms->kqs/dot_general | solution.py:43
  237.9 6.6 %add_bitcast_fusion = (f32[64,64,256]{2,1,0:T(8,128)S(1)}, f32[64,64,256]{2,1,0:T(8,128)S(1)}) fusion(f32[64,256,64]{1,2,0:T(8,128)S(1)} %fusion.44, f32[64,64]{1,0:T(8,128)S(1)} %get-tuple-element.24, f32[64,64]{1,0:T(8,128)S(1)} %get-tuple-element.25, f32[64,256,64]{1,2,0:T(8,128)S(1)} %fusion, f32[64,256,64]{1,2,0:T(8,128)S(1)} %get-tuple-element.10), kind=kOutput, calls=%fused_computation.12 | convolution fusion | flops 812703744 | bytes 21004288 | tf_op jit(solution)/shard_map/mq,kqs->kms/dot_general | solution.py:43
  249.2 5.0 %fusion.10 = f32[32,64,256]{2,0,1:T(8,128)S(1)} fusion(f32[64,64,256]{2,1,0:T(8,128)S(1)} %get-tuple-element.13), kind=kOutput, calls=%fused_computation.21 | convolution fusion | flops 402681856 | bytes 6291456 | tf_op jit(solution)/shard_map/nk,kms->nms/dot_general | solution.py:43
  254.2 4.8 %multiply_convert_fusion.1 = bf16[32,64,256]{2,0,1:T(8,128)(2,1)S(1)} fusion(f32[32,64,256]{2,0,1:T(8,128)S(1)} %fusion.10, f32[64,64,256]{2,1,0:T(8,128)S(1)} %get-tuple-element.12), kind=kOutput, calls=%fused_computation.72 | convolution fusion | flops 405303296 | bytes 7340032 | tf_op jit(solution)/shard_map/nk,kms->nms/dot_general | solution.py:43
  258.9 4.9 %multiply_convert_fusion = bf16[32,64,256]{2,0,1:T(8,128)(2,1)S(1)} fusion(f32[32,64,256]{2,0,1:T(8,128)S(1)} %fusion.8, f32[64,64,256]{2,1,0:T(8,128)S(1)} %get-tuple-element.12), kind=kOutput, calls=%fused_computation.71 | convolution fusion | flops 404254720 | bytes 7340032 | tf_op jit(solution)/shard_map/nk,kms->nms/dot_general | solution.py:40
  270.8 55.8 %all_to_all.48 = bf16[1,2048,2,2,128]{4,3,2,0,1:T(2,128)(2,1)S(1)} all-to-all(bf16[1,2048,2,2,128]{4,3,2,0,1:T(2,128)(2,1)S(1)} %copy.132), channel_id=1, replica_groups=mesh['len'=4,'eng'=64] {'eng'}, dimensions={1} | all-to-all | bytes 4194304 | tf_op jit(solution)/shard_map/all_to_all | solution.py:133
  330.3 6.4 %collective-permute-start.2 = (bf16[1,32,2,128,128]{3,4,2,1,0:T(8,128)(2,1)}, bf16[1,32,2,128,128]{3,4,2,1,0:T(8,128)(2,1)S(1)}, u32[]{:S(2)}, u32[]{:S(2)}) collective-permute-start(bf16[1,32,2,128,128]{3,4,2,1,0:T(8,128)(2,1)} %copy.135), channel_id=1, source_target_pairs={{64,0},{128,64},{192,128},{65,1},{129,65},{193,129},{66,2},{130,66... | collective-permute-start | bytes 6291464 | tf_op jit(solution)/shard_map/ppermute | solution.py:21
  345.2 5.3 %collective-permute-start = (bf16[1,32,2,128,128]{3,4,2,1,0:T(8,128)(2,1)S(1)}, bf16[1,32,2,128,128]{3,4,2,1,0:T(8,128)(2,1)}, u32[]{:S(2)}, u32[]{:S(2)}) collective-permute-start(bf16[1,32,2,128,128]{3,4,2,1,0:T(8,128)(2,1)S(1)} %copy-done), channel_id=1, source_target_pairs={{0,64},{64,128},{128,192},{1,65},{65,129},{129,193},{2,66},{66,130... | collective-permute-start | bytes 6291464 | tf_op jit(solution)/shard_map/ppermute | solution.py:19
  355.7 7.4 %collective-permute-done.2 = bf16[1,32,2,128,128]{3,4,2,1,0:T(8,128)(2,1)S(1)} collective-permute-done((bf16[1,32,2,128,128]{3,4,2,1,0:T(8,128)(2,1)}, bf16[1,32,2,128,128]{3,4,2,1,0:T(8,128)(2,1)S(1)}, u32[]{:S(2)}, u32[]{:S(2)}) %collective-permute-start.2) | collective-permute-done | bytes 2097184 | tf_op jit(solution)/shard_map/ppermute | solution.py:21
  367.4 5.9 %collective-permute-done = bf16[1,32,2,128,128]{3,4,2,1,0:T(8,128)(2,1)} collective-permute-done((bf16[1,32,2,128,128]{3,4,2,1,0:T(8,128)(2,1)S(1)}, bf16[1,32,2,128,128]{3,4,2,1,0:T(8,128)(2,1)}, u32[]{:S(2)}, u32[]{:S(2)}) %collective-permute-start) | collective-permute-done | bytes 2097184 | tf_op jit(solution)/shard_map/ppermute | solution.py:19
  373.3 6.8 %fusion.79 = bf16[1,32,2,128,128]{4,3,2,1,0:T(8,128)(2,1)} fusion(f32[32,2,128,128]{3,2,1,0:T(8,128)} %fusion.52, f32[32,2,128,128]{3,2,1,0:T(8,128)} %fusion.56, bf16[1,32,2,128,128]{3,4,2,1,0:T(8,128)(2,1)} %collective-permute-done, bf16[1,2,128,128]{3,2,1,0:T(8,128)(2,1)S(1)} %collective-permute-done.1), kind=kOutput, calls=%fused_computation.75 | convolution fusion | flops 541065216 | bytes 12648448 | tf_op jit(solution)/shard_map/recij,rjk->recik/dot_general | solution.py:123
  (48 shorter events, 99.0 us)
Async XLA Ops:
  4.9 61.9 %all-to-all-start = ((bf16[1,32,2,128,128]{4,1,2,0,3:T(8,128)(2,1)}), bf16[1,32,2,128,128]{4,1,2,0,3:T(8,128)(2,1)S(1)}, u32[]{:S(2)}, u32[]{:S(2)}) async-start(bf16[1,32,2,128,128]{4,1,2,0,3:T(8,128)(2,1)} %copy.104), calls=%async_computation | async-start | bytes 4194304 | tf_op jit(solution)/shard_map/all_to_all | solution.py:129
  66.8 54.9 %all-to-all-start.1 = ((bf16[1,32,2,128,128]{4,1,2,0,3:T(8,128)(2,1)}), bf16[1,32,2,128,128]{4,1,2,0,3:T(8,128)(2,1)}, u32[]{:S(2)}, u32[]{:S(2)}) async-start(bf16[1,32,2,128,128]{4,1,2,0,3:T(8,128)(2,1)} %copy.114), calls=%async_computation.1 | async-start | bytes 4194304 | tf_op jit(solution)/shard_map/all_to_all | solution.py:130
  326.8 9.9 %copy-start.1 = (bf16[1,2,128,128]{3,2,1,0:T(8,128)(2,1)S(1)}, bf16[1,2,128,128]{3,2,1,0:T(8,128)(2,1)}, u32[]{:S(2)}) copy-start(bf16[1,2,128,128]{3,2,1,0:T(8,128)(2,1)} %param.5) | copy-start | bytes 196612
  330.3 15.0 %copy-start = (bf16[1,32,2,128,128]{3,4,2,1,0:T(8,128)(2,1)S(1)}, bf16[1,32,2,128,128]{3,4,2,1,0:T(8,128)(2,1)}, u32[]{:S(2)}) copy-start(bf16[1,32,2,128,128]{3,4,2,1,0:T(8,128)(2,1)} %copy.135) | copy-start | bytes 6291460
  330.3 32.9 %collective-permute-start.2 = (bf16[1,32,2,128,128]{3,4,2,1,0:T(8,128)(2,1)}, bf16[1,32,2,128,128]{3,4,2,1,0:T(8,128)(2,1)S(1)}, u32[]{:S(2)}, u32[]{:S(2)}) collective-permute-start(bf16[1,32,2,128,128]{3,4,2,1,0:T(8,128)(2,1)} %copy.135), channel_id=1, source_target_pairs={{64,0},{128,64},{192,128},{65,1},{129,65},{193,129},{66,2},{130,66... | collective-permute-start | bytes 6291464 | tf_op jit(solution)/shard_map/ppermute | solution.py:21
  336.7 30.6 %collective-permute-start.1 = (bf16[1,2,128,128]{3,2,1,0:T(8,128)(2,1)S(1)}, bf16[1,2,128,128]{3,2,1,0:T(8,128)(2,1)S(1)}, u32[]{:S(2)}, u32[]{:S(2)}) collective-permute-start(bf16[1,2,128,128]{3,2,1,0:T(8,128)(2,1)S(1)} %copy-done.1), channel_id=1, source_target_pairs={{0,64},{64,128},{128,192},{1,65},{65,129},{129,193},{2,66},{66,130... | collective-permute-start | bytes 196616 | tf_op jit(solution)/shard_map/ppermute | solution.py:19
  341.2 25.5 %collective-permute-start.3 = (bf16[1,2,128,128]{3,2,1,0:T(8,128)(2,1)S(1)}, bf16[1,2,128,128]{3,2,1,0:T(8,128)(2,1)S(1)}, u32[]{:S(2)}, u32[]{:S(2)}) collective-permute-start(bf16[1,2,128,128]{3,2,1,0:T(8,128)(2,1)S(1)} %copy-done.1), channel_id=1, source_target_pairs={{64,0},{128,64},{192,128},{65,1},{129,65},{193,129},{66,2},{130,66... | collective-permute-start | bytes 196616 | tf_op jit(solution)/shard_map/ppermute | solution.py:21
  345.2 28.1 %collective-permute-start = (bf16[1,32,2,128,128]{3,4,2,1,0:T(8,128)(2,1)S(1)}, bf16[1,32,2,128,128]{3,4,2,1,0:T(8,128)(2,1)}, u32[]{:S(2)}, u32[]{:S(2)}) collective-permute-start(bf16[1,32,2,128,128]{3,4,2,1,0:T(8,128)(2,1)S(1)} %copy-done), channel_id=1, source_target_pairs={{0,64},{64,128},{128,192},{1,65},{65,129},{129,193},{2,66},{66,130... | collective-permute-start | bytes 6291464 | tf_op jit(solution)/shard_map/ppermute | solution.py:19
where the time goes:
time: 389 us; the launch traced here: 384 us
  matrix products  146 us (38%)
  waiting for transfers between devices  93.1 us (24%)
  blocking collectives  55.8 us (14%)
  local copies, waits for them, and re-layouts  41.2 us (11%)
  starting transfers between devices  39.7 us (10%)
  other arithmetic  7.6 us (2%)
    all_to_all x1, blocking collectives, body(): lax.all_to_all(polar, 'eng', split_axis=1, concat_axis=3, tiled=True)  55.8 us
    all_to_all x1, waiting for transfers between devices, body(): lax.all_to_all(less_green, 'eng', split_axis=3, concat_axis=1, tiled=True)  44.2 us
    dot_general x6, matrix products, complex_mix(): jnp.einsum(pattern, left_pair[1], right_pair[0], precision=highest)  42 us
    all_to_all x1, waiting for transfers between devices, body(): lax.all_to_all(greater_green, 'eng', split_axis=3, concat_axis=1, tiled=T...  35.6 us
    dot_general x6, matrix products, complex_mix(): jnp.einsum(pattern, left_pair[1], right_pair[1], precision=highest)  30.9 us
    dot_general x6, matrix products, complex_mix(): jnp.einsum(pattern, left_pair[0], right_pair[1], precision=highest)  28.8 us
    dot_general x6, matrix products, complex_mix(): jnp.einsum(pattern, left_pair[0], right_pair[0], precision=highest)  27.9 us
    dot_general x5, matrix products, right_apply(): jnp.einsum(pattern, fields, matrix, preferred_element_type=jnp.float32)  13.8 us
  transfers between devices with their start and end apart: 6, of which 4 were waited for; matrix products, arithmetic and copies ran while one was open for 7% of the time, Pallas kernels for 0%

commit v1 on v0

v1 whole, which is shorter than its diff:
```python
import math

import jax
import jax.numpy as jnp
import ml_dtypes
import numpy as np
from jax import lax
from jax.experimental import pallas as pl
from jax.experimental.pallas import tpu as pltpu
from jax.sharding import PartitionSpec as P

F32 = jnp.float32
BF16 = jnp.bfloat16

ENERGIES = 2048
SLOTS = 64
LOCAL = ENERGIES // SLOTS
SIDE = 128
HALF = SIDE // SLOTS
OUTER = 2 * SLOTS
MIB = 1024 * 1024


def halves(table):
    high = table.astype(np.float32).astype(ml_dtypes.bfloat16)
    low = (table - high.astype(np.float64)).astype(np.float32).astype(ml_dtypes.bfloat16)
    return high, low


def real_form(table):
    top = np.concatenate([table.real, -table.imag], axis=-1)
    bottom = np.concatenate([table.imag, table.real], axis=-1)
    return np.concatenate([top, bottom], axis=-2)


def dft_tables():
    period = 2 * ENERGIES
    outer = np.arange(OUTER)
    slow = np.arange(SLOTS)
    fast = np.arange(LOCAL)
    turn = 2j * np.pi
    first = real_form(np.exp(-turn * ((outer[:, None] * slow[None, :]) % OUTER) / OUTER))
    freq = outer[:, None, None] + OUTER * fast[None, :, None]
    phase = (freq * fast[None, None, :]) % period
    second = real_form(np.exp(-turn * phase / period))
    third = real_form(np.exp(turn * np.swapaxes(phase, 1, 2) / period))
    last = np.exp(turn * ((slow[:, None] * outer[None, :]) % OUTER) / OUTER)
    last = real_form(1j * last / (period * math.sqrt(ENERGIES)))
    first_hi, first_lo = halves(first)
    second_hi, second_lo = halves(second)
    third_hi, third_lo = halves(third)
    last_hi, last_lo = halves(last)
    return (
        np.concatenate([first_hi, first_lo], axis=1),
        np.concatenate([second_hi, second_lo, second_hi], axis=2),
        np.concatenate([third_hi, third_lo, third_hi], axis=2),
        np.concatenate([last_hi, last_lo], axis=0),
    )


TABLES = dft_tables()


def split(values):
    high = values.astype(BF16)
    return high, (values - high.astype(F32)).astype(BF16)


def mm(left, right):
    return jnp.dot(left, right, preferred_element_type=F32)


def pack_kernel(in_ref, out_ref, wide):
    def fill(n, carry):
        for part in range(2):
            start = pl.multiple_of((part * LOCAL + n) * SLOTS, SLOTS)
            wide[pl.ds(start, SLOTS), :] = in_ref[0, n, part].astype(F32)
        return carry

    def emit(row, carry):
        out_ref[row, 0] = wide[pl.ds(row, 2 * LOCAL, stride=SLOTS), :].astype(BF16)
        return carry

    lax.fori_loop(0, LOCAL, fill, 0, unroll=4)
    lax.fori_loop(0, SLOTS, emit, 0, unroll=4)


def pack(green):
    return pl.pallas_call(
        pack_kernel,
        grid=(HALF,),
        out_shape=jax.ShapeDtypeStruct((SLOTS, HALF, 2 * LOCAL, SIDE), BF16),
        in_specs=[pl.BlockSpec((1, LOCAL, 2, SLOTS, SIDE), lambda c: (0, 0, 0, c, 0))],
        out_specs=pl.BlockSpec((SLOTS, 1, 2 * LOCAL, SIDE), lambda c: (0, c, 0, 0)),
        scratch_shapes=[pltpu.VMEM((2 * LOCAL * SLOTS, SIDE), F32)],
        compiler_params=pltpu.CompilerParams(vmem_limit_bytes=24 * MIB),
        name="pack",
    )(green)


def unpack_kernel(in_ref, out_ref, wide):
    def fill(row, carry):
        start = pl.multiple_of(row * 2 * LOCAL, 2 * LOCAL)
        wide[pl.ds(start, 2 * LOCAL), :] = in_ref[row, 0].astype(F32)
        return carry

    def emit(n, carry):
        for part in range(2):
            line = wide[pl.ds(part * LOCAL + n, SLOTS, stride=2 * LOCAL), :]
            out_ref[0, n, part] = line.astype(BF16)
        return carry

    lax.fori_loop(0, SLOTS, fill, 0, unroll=4)
    lax.fori_loop(0, LOCAL, emit, 0, unroll=4)


def unpack(parcels):
    return pl.pallas_call(
        unpack_kernel,
        grid=(HALF,),
        out_shape=jax.ShapeDtypeStruct((1, LOCAL, 2, SIDE, SIDE), BF16),
        in_specs=[pl.BlockSpec((SLOTS, 1, 2 * LOCAL, SIDE), lambda c: (0, c, 0, 0))],
        out_specs=pl.BlockSpec((1, LOCAL, 2, SLOTS, SIDE), lambda c: (0, 0, 0, c, 0)),
        scratch_shapes=[pltpu.VMEM((2 * LOCAL * SLOTS, SIDE), F32)],
        compiler_params=pltpu.CompilerParams(vmem_limit_bytes=24 * MIB),
        name="unpack",
    )(parcels)


def correlate_kernel(g_ref, h_ref, w1_ref, w2_ref, w3_ref, w4_ref, out_ref, wide, mid, back, tail):
    chunk = 2 * LOCAL

    def fill(source, carry):
        start = pl.multiple_of(source * chunk, chunk)
        wide[0, pl.ds(start, chunk), :] = g_ref[source, 0].astype(F32)
        wide[1, pl.ds(start, chunk), :] = h_ref[source, 0].astype(F32)
        return carry

    def first(n, carry):
        cols = [
            jnp.concatenate(
                [
                    wide[which, pl.ds(part * LOCAL + n, SLOTS, stride=chunk), :]
                    for part in range(2)
                ],
                axis=0,
            ).astype(BF16)
            for which in range(2)
        ]
        x = jnp.concatenate(cols, axis=1)
        y = mm(w1_ref[...], jnp.concatenate([x, x], axis=0))
        start = pl.multiple_of(n * 2 * OUTER, 2 * OUTER)
        mid[0, pl.ds(start, 2 * OUTER), :] = y[:, :SIDE]
        mid[1, pl.ds(start, 2 * OUTER), :] = y[:, SIDE:]
        return carry

    def middle(k, carry):
        cols = [
            jnp.concatenate(
                [
                    mid[which, pl.ds(part * OUTER + k, LOCAL, stride=2 * OUTER), :]
                    for part in range(2)
                ],
                axis=0,
            )
            for which in range(2)
        ]
        high, low = split(jnp.concatenate(cols, axis=1))
        z = mm(w2_ref[k], jnp.concatenate([high, high, low], axis=0))
        g_re, g_im = z[:LOCAL, :SIDE], z[LOCAL:, :SIDE]
        h_re, h_im = z[:LOCAL, SIDE:], z[LOCAL:, SIDE:]
        product = jnp.concatenate([g_re * h_re + g_im * h_im, g_im * h_re - g_re * h_im], axis=0)
        high, low = split(product)
        start = pl.multiple_of(k * chunk, chunk)
        back[pl.ds(start, chunk), :] = mm(w3_ref[k], jnp.concatenate([high, high, low], axis=0))
        return carry

    def last(pair, carry):
        lines = [
            jnp.concatenate(
                [
                    back[pl.ds(part * LOCAL + 2 * pair + which, OUTER, stride=chunk), :]
                    for part in range(2)
                ],
                axis=0,
            )
            for which in range(2)
        ]
        high, low = split(jnp.concatenate(lines, axis=1))
        both = mm(w4_ref[...], high)
        y = both[:OUTER] + both[OUTER:] + mm(w4_ref[:OUTER, :], low)
        start = pl.multiple_of(pair * 2 * OUTER, 2 * OUTER)
        tail[pl.ds(start, OUTER), :] = y[:, :SIDE]
        tail[pl.ds(start + OUTER, OUTER), :] = y[:, SIDE:]
        return carry

    def emit(slot, carry):
        for part in range(2):
            line = tail[pl.ds(part * SLOTS + slot, LOCAL, stride=OUTER), :]
            out_ref[slot, 0, part * LOCAL : (part + 1) * LOCAL, :] = line.astype(BF16)
        return carry

    lax.fori_loop(0, SLOTS, fill, 0, unroll=4)
    lax.fori_loop(0, LOCAL, first, 0, unroll=2)
    lax.fori_loop(0, OUTER, middle, 0, unroll=4)
    lax.fori_loop(0, LOCAL // 2, last, 0, unroll=2)
    lax.fori_loop(0, SLOTS, emit, 0, unroll=4)


def correlate(less, greater, tables):
    parcel = pl.BlockSpec((SLOTS, 1, 2 * LOCAL, SIDE), lambda c: (0, c, 0, 0))
    whole = [
        pl.BlockSpec(t.shape, lambda c, rank=t.ndim: (0,) * rank, pipeline_mode=pl.Buffered(1))
        for t in tables
    ]
    return pl.pallas_call(
        correlate_kernel,
        grid=(HALF,),
        out_shape=jax.ShapeDtypeStruct((SLOTS, HALF, 2 * LOCAL, SIDE), BF16),
        in_specs=[parcel, parcel, *whole],
        out_specs=parcel,
        scratch_shapes=[
            pltpu.VMEM((2, ENERGIES * 2, SIDE), F32),
            pltpu.VMEM((2, LOCAL * 2 * OUTER, SIDE), F32),
            pltpu.VMEM((OUTER * 2 * LOCAL, SIDE), F32),
            pltpu.VMEM((LOCAL * OUTER, SIDE), F32),
        ],
        compiler_params=pltpu.CompilerParams(vmem_limit_bytes=52 * MIB),
        name="correlate",
    )(less, greater, *tables)


SPAN = 8


def screen_kernel(lower_ref, own_ref, upper_ref, left_ref, right_ref, out_ref):
    def step(n, carry):
        fields = []
        for which, ref in enumerate((lower_ref, own_ref, upper_ref)):
            both = jnp.concatenate([ref[0, n, 0], ref[0, n, 1]], axis=1)
            fields.append(mm(left_ref[which], both).astype(BF16))
        for part in range(2):
            cols = slice(part * SIDE, (part + 1) * SIDE)
            row = jnp.concatenate([field[:, cols] for field in fields], axis=1)
            result = mm(row, right_ref[...]).astype(BF16)
            out_ref[0, n, part] = result[:, :SIDE]
            out_ref[0, n, 2 + part] = result[:, SIDE:]
        return carry

    lax.fori_loop(0, SPAN, step, 0, unroll=2)


def screen(lower, own, upper, left, right):
    field = pl.BlockSpec((1, SPAN, 2, SIDE, SIDE), lambda s: (0, s, 0, 0, 0))
    return pl.pallas_call(
        screen_kernel,
        grid=(LOCAL // SPAN,),
        out_shape=jax.ShapeDtypeStruct((1, LOCAL, 4, SIDE, SIDE), BF16),
        in_specs=[
            field,
            field,
            field,
            pl.BlockSpec(left.shape, lambda s: (0, 0, 0)),
            pl.BlockSpec(right.shape, lambda s: (0, 0)),
        ],
        out_specs=pl.BlockSpec((1, SPAN, 4, SIDE, SIDE), lambda s: (0, s, 0, 0, 0)),
        compiler_params=pltpu.CompilerParams(vmem_limit_bytes=32 * MIB),
        name="screen",
    )(lower, own, upper, left, right)


def from_below(cells):
    ends = lax.axis_size("len") - 1
    return lax.ppermute(cells, "len", [(i, i + 1) for i in range(ends)])


def from_above(cells):
    ends = lax.axis_size("len") - 1
    return lax.ppermute(cells, "len", [(i + 1, i) for i in range(ends)])


def exchange(parcels):
    return lax.all_to_all(parcels, "eng", split_axis=0, concat_axis=0, tiled=True)


def coefficients(coulomb):
    own_diag, own_up = coulomb[0, 0], coulomb[0, 1]
    prev_up = from_below(coulomb[:, 1])[0]
    next_diag = from_above(coulomb[:, 0])[0]
    left = jnp.stack([prev_up.T, own_diag, own_up])
    right = jnp.concatenate(
        [
            jnp.concatenate([prev_up, jnp.zeros_like(prev_up)], axis=1),
            jnp.concatenate([own_diag, own_up], axis=1),
            jnp.concatenate([own_up.T, next_diag], axis=1),
        ],
        axis=0,
    )
    return left, right


def body(less_green, greater_green, coulomb):
    left, right = coefficients(coulomb)
    tables = [jnp.asarray(table) for table in TABLES]
    less = exchange(pack(less_green))
    greater = exchange(pack(greater_green))
    polar = unpack(exchange(correlate(less, greater, tables)))
    screened = screen(from_below(polar), polar, from_above(polar), left, right)
    return polar, screened


def solution(mesh):
    in_specs = (
        P("len", "eng", None, None, None),
        P("len", "eng", None, None, None),
        P("len", None, None, None),
    )
    out_specs = (P("len", "eng", None, None, None), P("len", "eng", None, None, None))
    return jax.shard_map(body, mesh=mesh, in_specs=in_specs, out_specs=out_specs, check_vma=False)
```

time: 389 us -> 296 us (0.76)
  matrix products: 146 us -> 0 us
  Pallas kernels: 0 us -> 87.9 us
  blocking collectives: 55.8 us -> 110 us
  local copies, waits for them, and re-layouts: 41.2 us -> 5.02 us
  waiting for transfers between devices: 93.1 us -> 62 us
  starting transfers between devices: 39.7 us -> 28.9 us
  other arithmetic: 7.6 us -> 0.04 us
    dot_general x31 -> x0, matrix products: 146 us -> none  [the longest x6 42 us: complex_mix(): jnp.einsum(pattern, left_pair[1], right_pair[0], precision=highest)]
    pallas_call x0 -> x5, Pallas kernels: none -> 87.9 us  [the longest x1 64 us: correlate(): pl.pallas_call(correlate_kernel, grid=(HALF,), out_shape=jax.ShapeDtypeSt...]
    all_to_all x1 -> x2, blocking collectives: 55.8 us -> 110 us  [exchange(): lax.all_to_all(parcels, 'eng', split_axis=0, concat_axis=0, tiled=True)]
    all_to_all x2 -> x1, waiting for transfers between devices: 79.7 us -> 43.1 us  [exchange(): lax.all_to_all(parcels, 'eng', split_axis=0, concat_axis=0, tiled=True)]
    all_to_all x5 -> x0, local copies, waits for them, and re-layouts: 14.4 us -> none  [the longest x1 6.15 us: body(): lax.all_to_all(greater_green, 'eng', split_axis=3, concat_axis=1, tiled=T...]
    another operation x7 -> x1, local copies, waits for them, and re-layouts: 12.7 us -> 0.11 us  [coefficients(): left = jnp.stack([prev_up.T, own_diag, own_up])]
    all_to_all x2 -> x1, starting transfers between devices: 21.6 us -> 13.8 us  [exchange(): lax.all_to_all(parcels, 'eng', split_axis=0, concat_axis=0, tiled=True)]
    unnamed x7 -> x12, local copies, waits for them, and re-layouts: 10.7 us -> 4.77 us
  transfers between devices with their start and end apart: 6 -> 5, of which waited for: 4 -> 2; matrix products, arithmetic and copies ran while one was open for 7% -> 0% of each run, Pallas kernels for 0% -> 1%
where the time goes in v1:
time: 296 us; the launch traced here: 295 us
  blocking collectives  110 us (37%)
  Pallas kernels  87.9 us (30%)
  waiting for transfers between devices  62 us (21%)
  starting transfers between devices  28.9 us (10%)
  local copies, waits for them, and re-layouts  5.02 us (2%)
    all_to_all x2, blocking collectives, exchange(): lax.all_to_all(parcels, 'eng', split_axis=0, concat_axis=0, tiled=True)  110 us
    pallas_call x1, Pallas kernels, correlate(): pl.pallas_call(correlate_kernel, grid=(HALF,), out_shape=jax.ShapeDtypeSt...  64 us
    all_to_all x1, waiting for transfers between devices, exchange(): lax.all_to_all(parcels, 'eng', split_axis=0, concat_axis=0, tiled=True)  43.1 us
    ppermute x2, waiting for transfers between devices, from_below(): return lax.ppermute(cells, 'len', [(i, i + 1) for i in range(ends)])  18.9 us
    all_to_all x1, starting transfers between devices, exchange(): lax.all_to_all(parcels, 'eng', split_axis=0, concat_axis=0, tiled=True)  13.8 us
    pallas_call x1, Pallas kernels, screen(): pl.pallas_call(screen_kernel, grid=(LOCAL // SPAN,), out_shape=jax.ShapeD...  10.8 us
    ppermute x2, starting transfers between devices, from_above(): return lax.ppermute(cells, 'len', [(i + 1, i) for i in range(ends)])  8.2 us
    pallas_call x2, Pallas kernels, pack(): pl.pallas_call(pack_kernel, grid=(HALF,), out_shape=jax.ShapeDtypeStruct(...  8.02 us
  transfers between devices with their start and end apart: 5, of which 2 were waited for; matrix products, arithmetic and copies ran while one was open for 0% of the time, Pallas kernels for 1%

profile of v1, /device:TPU:1, one launch (start us, length us, event | category | flops | bytes accessed | tf_op | source)
XLA Modules:
  0.0 295.2 jit_solution(2633883556869379568)
XLA Ops:
  0.6 1.6 copy-done.1
  2.2 4.4 %pack.2 = bf16[64,2,64,128]{3,2,1,0:T(8,128)(2,1)} custom-call(bf16[1,32,2,128,128]{4,3,2,1,0:T(8,128)(2,1)S(1)} %copy-done.1), custom_call_target="tpu_custom_call" | custom-call | tf_op jit(solution)/shard_map/pack/pallas_call | solution.py:89
  6.7 13.8 %all-to-all-start = ((bf16[64,2,64,128]{3,2,1,0:T(8,128)(2,1)}), bf16[64,2,64,128]{3,2,1,0:T(8,128)(2,1)}, u32[]{:S(2)}, u32[]{:S(2)}) async-start(bf16[64,2,64,128]{3,2,1,0:T(8,128)(2,1)} %pack.2), calls=%async_computation | async-start | bytes 4194304 | tf_op jit(solution)/shard_map/all_to_all | solution.py:283
  20.4 0.0 copy-start.2
  20.4 1.6 copy-done.2
  22.0 3.6 %pack.3 = bf16[64,2,64,128]{3,2,1,0:T(8,128)(2,1)S(1)} custom-call(bf16[1,32,2,128,128]{4,3,2,1,0:T(8,128)(2,1)S(1)} %copy-done.2), custom_call_target="tpu_custom_call" | custom-call | tf_op jit(solution)/shard_map/pack/pallas_call | solution.py:89
  25.6 0.0 copy-start.3
  25.6 0.0 copy-start.4
  25.6 43.1 %all-to-all-done.g_ref = bf16[64,2,64,128]{3,2,1,0:T(8,128)(2,1)} async-done(((bf16[64,2,64,128]{3,2,1,0:T(8,128)(2,1)}), bf16[64,2,64,128]{3,2,1,0:T(8,128)(2,1)}, u32[]{:S(2)}, u32[]{:S(2)}) %all-to-all-start) | async-done | bytes 2097184 | tf_op jit(solution)/shard_map/all_to_all | solution.py:283
  68.7 54.5 %all_to_all.15.h_ref = bf16[64,2,64,128]{3,2,1,0:T(8,128)(2,1)} all-to-all(bf16[64,2,64,128]{3,2,1,0:T(8,128)(2,1)S(1)} %pack.3), channel_id=1, replica_groups=mesh['len'=4,'eng'=64] {'eng'}, dimensions={0} | all-to-all | bytes 4194304 | tf_op jit(solution)/shard_map/all_to_all | solution.py:283
  123.2 64.0 %correlate.1 = bf16[64,2,64,128]{3,2,1,0:T(8,128)(2,1)} custom-call(bf16[64,2,64,128]{3,2,1,0:T(8,128)(2,1)} %all-to-all-done.g_ref, bf16[64,2,64,128]{3,2,1,0:T(8,128)(2,1)} %all_to_all.15.h_ref, bf16[256,256]{1,0:T(8,128)(2,1)S(1)} %copy-done.4, bf16[128,64,192]{2,1,0:T(8,128)(2,1)} %constant.11.clone.w2_ref, bf16[128,64,192]{2,1,0:T(8,128)(2,1)} %constant.12.clone.w3_ref, ...), custom_call_target="tpu_custom_call" | custom-call | tf_op jit(solution)/shard_map/correlate/pallas_call | solution.py:216
  187.2 56.0 %all_to_all.16.in_ref = bf16[64,2,64,128]{3,2,1,0:T(8,128)(2,1)S(1)} all-to-all(bf16[64,2,64,128]{3,2,1,0:T(8,128)(2,1)} %correlate.1), channel_id=1, replica_groups=mesh['len'=4,'eng'=64] {'eng'}, dimensions={0} | all-to-all | bytes 4194304 | tf_op jit(solution)/shard_map/all_to_all | solution.py:283
  243.2 5.1 %unpack.1.own_ref = bf16[1,32,2,128,128]{4,3,2,1,0:T(8,128)(2,1)} custom-call(bf16[64,2,64,128]{3,2,1,0:T(8,128)(2,1)S(1)} %all_to_all.16.in_ref), custom_call_target="tpu_custom_call" | custom-call | tf_op jit(solution)/shard_map/unpack/pallas_call | solution.py:118
  248.3 6.3 %collective-permute-start.1 = (bf16[1,32,2,128,128]{4,3,2,1,0:T(8,128)(2,1)}, bf16[1,32,2,128,128]{4,3,2,1,0:T(8,128)(2,1)S(1)}, u32[]{:S(2)}, u32[]{:S(2)}) collective-permute-start(bf16[1,32,2,128,128]{4,3,2,1,0:T(8,128)(2,1)} %unpack.1.own_ref), channel_id=1, source_target_pairs={{64,0},{128,64},{192,128},{65,1},{129,65},{193,129},{66,2},{130,66... | collective-permute-start | bytes 6291464 | tf_op jit(solution)/shard_map/ppermute | solution.py:279
  254.6 4.4 %collective-permute-start = (bf16[1,32,2,128,128]{4,3,2,1,0:T(8,128)(2,1)}, bf16[1,32,2,128,128]{4,3,2,1,0:T(8,128)(2,1)}, u32[]{:S(2)}, u32[]{:S(2)}) collective-permute-start(bf16[1,32,2,128,128]{4,3,2,1,0:T(8,128)(2,1)} %unpack.1.own_ref), channel_id=1, source_target_pairs={{0,64},{64,128},{128,192},{1,65},{65,129},{129,193},{2,66},{66,130... | collective-permute-start | bytes 6291464 | tf_op jit(solution)/shard_map/ppermute | solution.py:274
  259.1 2.5 collective-permute-start.2
  261.6 1.9 collective-permute-start.3
  263.5 0.1 copy.10
  263.7 18.9 %collective-permute-done.2 = bf16[1,128,128]{2,1,0:T(8,128)(2,1)S(1)} collective-permute-done((bf16[1,128,128]{2,1,0:T(8,128)(2,1)S(1)}, bf16[1,128,128]{2,1,0:T(8,128)(2,1)S(1)}, u32[]{:S(2)}, u32[]{:S(2)}) %collective-permute-start.2) | collective-permute-done | bytes 32800 | tf_op jit(solution)/shard_map/ppermute | solution.py:274
  282.5 0.1 copy.9
  282.7 0.0 collective-permute-done.3
  282.7 0.0 copy-start
  282.8 1.6 copy-done
  284.3 10.8 %screen.1 = bf16[1,32,4,128,128]{4,3,2,1,0:T(8,128)(2,1)} custom-call(bf16[1,32,2,128,128]{4,3,2,1,0:T(8,128)(2,1)} %collective-permute-done.lower_ref, bf16[1,32,2,128,128]{4,3,2,1,0:T(8,128)(2,1)S(1)} %copy-done, bf16[1,32,2,128,128]{4,3,2,1,0:T(8,128)(2,1)S(1)} %collective-permute-done.1.upper_ref, bf16[3,128,128]{2,1,0:T(8,128)(2,1)S(1)} %pad_maximum_fusion.left_ref, ...), custom_call_target="tpu_custom_call" | custom-call | tf_op jit(solution)/shard_map/screen/pallas_call | solution.py:255
  (10 shorter events, 0.1 us)
Async XLA Ops:
  0.6 1.6 copy-start.1
  6.7 62.1 %all-to-all-start = ((bf16[64,2,64,128]{3,2,1,0:T(8,128)(2,1)}), bf16[64,2,64,128]{3,2,1,0:T(8,128)(2,1)}, u32[]{:S(2)}, u32[]{:S(2)}) async-start(bf16[64,2,64,128]{3,2,1,0:T(8,128)(2,1)} %pack.2), calls=%async_computation | async-start | bytes 4194304 | tf_op jit(solution)/shard_map/all_to_all | solution.py:283
  20.4 1.6 copy-start.2
  25.6 97.6 %copy-start.3 = (bf16[256,256]{1,0:T(8,128)(2,1)S(1)}, bf16[256,256]{1,0:T(8,128)(2,1)}, u32[]{:S(2)}) copy-start(bf16[256,256]{1,0:T(8,128)(2,1)} %constant.13.clone.w4_ref) | copy-start | bytes 393220
  25.6 97.6 %copy-start.4 = (bf16[256,256]{1,0:T(8,128)(2,1)S(1)}, bf16[256,256]{1,0:T(8,128)(2,1)}, u32[]{:S(2)}) copy-start(bf16[256,256]{1,0:T(8,128)(2,1)} %constant.10.clone.w1_ref) | copy-start | bytes 393220
  243.2 15.8 %copy-start.5 = (bf16[1,2,128,128]{3,2,1,0:T(8,128)(2,1)S(1)}, bf16[1,2,128,128]{3,2,1,0:T(8,128)(2,1)}, u32[]{:S(2)}) copy-start(bf16[1,2,128,128]{3,2,1,0:T(8,128)(2,1)} %param.9) | copy-start | bytes 196612
  248.3 34.4 %collective-permute-start.1 = (bf16[1,32,2,128,128]{4,3,2,1,0:T(8,128)(2,1)}, bf16[1,32,2,128,128]{4,3,2,1,0:T(8,128)(2,1)S(1)}, u32[]{:S(2)}, u32[]{:S(2)}) collective-permute-start(bf16[1,32,2,128,128]{4,3,2,1,0:T(8,128)(2,1)} %unpack.1.own_ref), channel_id=1, source_target_pairs={{64,0},{128,64},{192,128},{65,1},{129,65},{193,129},{66,2},{130,66... | collective-permute-start | bytes 6291464 | tf_op jit(solution)/shard_map/ppermute | solution.py:279
  254.6 28.2 %collective-permute-start = (bf16[1,32,2,128,128]{4,3,2,1,0:T(8,128)(2,1)}, bf16[1,32,2,128,128]{4,3,2,1,0:T(8,128)(2,1)}, u32[]{:S(2)}, u32[]{:S(2)}) collective-permute-start(bf16[1,32,2,128,128]{4,3,2,1,0:T(8,128)(2,1)} %unpack.1.own_ref), channel_id=1, source_target_pairs={{0,64},{64,128},{128,192},{1,65},{65,129},{129,193},{2,66},{66,130... | collective-permute-start | bytes 6291464 | tf_op jit(solution)/shard_map/ppermute | solution.py:274
  259.1 23.5 %collective-permute-start.2 = (bf16[1,128,128]{2,1,0:T(8,128)(2,1)S(1)}, bf16[1,128,128]{2,1,0:T(8,128)(2,1)S(1)}, u32[]{:S(2)}, u32[]{:S(2)}) collective-permute-start(bf16[1,128,128]{2,1,0:T(8,128)(2,1)S(1)} %get-tuple-element.6), channel_id=1, source_target_pairs={{0,64},{64,128},{128,192},{1,65},{65,129},{129,193},{2,66},{66,130... | collective-permute-start | bytes 98312 | tf_op jit(solution)/shard_map/ppermute | solution.py:274
  261.6 21.1 %collective-permute-start.3 = (bf16[1,128,128]{2,1,0:T(8,128)(2,1)S(1)}, bf16[1,128,128]{2,1,0:T(8,128)(2,1)S(1)}, u32[]{:S(2)}, u32[]{:S(2)}) collective-permute-start(bf16[1,128,128]{2,1,0:T(8,128)(2,1)S(1)} %get-tuple-element.5), channel_id=1, source_target_pairs={{64,0},{128,64},{192,128},{65,1},{129,65},{193,129},{66,2},{130,66... | collective-permute-start | bytes 98312 | tf_op jit(solution)/shard_map/ppermute | solution.py:279
  282.7 1.6 copy-start

commit v2 on v1

--- a/solution.py
+++ b/solution.py
@@ -70,38 +70,49 @@
     return jnp.dot(left, right, preferred_element_type=F32)
 
 
-def pack_kernel(in_ref, out_ref, wide):
+def pack_kernel(less_ref, greater_ref, out_ref, wide):
+    count = less_ref.shape[1]
+
     def fill(n, carry):
-        for part in range(2):
-            start = pl.multiple_of((part * LOCAL + n) * SLOTS, SLOTS)
-            wide[pl.ds(start, SLOTS), :] = in_ref[0, n, part].astype(F32)
+        for which, ref in enumerate((less_ref, greater_ref)):
+            for part in range(2):
+                start = pl.multiple_of(((which * 2 + part) * count + n) * SLOTS, SLOTS)
+                wide[pl.ds(start, SLOTS), :] = ref[0, n, part].astype(F32)
         return carry
 
     def emit(row, carry):
-        out_ref[row, 0] = wide[pl.ds(row, 2 * LOCAL, stride=SLOTS), :].astype(BF16)
-        return carry
-
-    lax.fori_loop(0, LOCAL, fill, 0, unroll=4)
-    lax.fori_loop(0, SLOTS, emit, 0, unroll=4)
-
-
-def pack(green):
+        for which in range(2):
+            for part in range(2):
+                start = (which * 2 + part) * count * SLOTS + row
+                line = wide[pl.ds(start, count, stride=SLOTS), :]
+                out_ref[row, which, part] = line.astype(BF16)
+        return carry
+
+    lax.fori_loop(0, count, fill, 0, unroll=4)
+    lax.fori_loop(0, SLOTS, emit, 0, unroll=8)
+
+
+def pack(less, greater, chunk):
+    steps = 2
+    count = LOCAL // steps
+    field = pl.BlockSpec((1, count, 2, SLOTS, SIDE), lambda s: (0, s, 0, chunk, 0))
     return pl.pallas_call(
         pack_kernel,
-        grid=(HALF,),
-        out_shape=jax.ShapeDtypeStruct((SLOTS, HALF, 2 * LOCAL, SIDE), BF16),
-        in_specs=[pl.BlockSpec((1, LOCAL, 2, SLOTS, SIDE), lambda c: (0, 0, 0, c, 0))],
-        out_specs=pl.BlockSpec((SLOTS, 1, 2 * LOCAL, SIDE), lambda c: (0, c, 0, 0)),
-        scratch_shapes=[pltpu.VMEM((2 * LOCAL * SLOTS, SIDE), F32)],
-        compiler_params=pltpu.CompilerParams(vmem_limit_bytes=24 * MIB),
+        grid=(steps,),
+        out_shape=jax.ShapeDtypeStruct((SLOTS, 2, 2, LOCAL, SIDE), BF16),
+        in_specs=[field, field],
+        out_specs=pl.BlockSpec((SLOTS, 2, 2, count, SIDE), lambda s: (0, 0, 0, s, 0)),
+        scratch_shapes=[pltpu.VMEM((4 * count * SLOTS, SIDE), F32)],
+        compiler_params=pltpu.CompilerParams(vmem_limit_bytes=60 * MIB),
+        cost_estimate=pl.CostEstimate(flops=0, bytes_accessed=8 * MIB, transcendentals=0),
         name="pack",
-    )(green)
+    )(less, greater)
 
 
 def unpack_kernel(in_ref, out_ref, wide):
     def fill(row, carry):
         start = pl.multiple_of(row * 2 * LOCAL, 2 * LOCAL)
-        wide[pl.ds(start, 2 * LOCAL), :] = in_ref[row, 0].astype(F32)
+        wide[pl.ds(start, 2 * LOCAL), :] = in_ref[row].astype(F32)
         return carry
 
     def emit(n, carry):
@@ -117,23 +128,22 @@
 def unpack(parcels):
     return pl.pallas_call(
         unpack_kernel,
-        grid=(HALF,),
-        out_shape=jax.ShapeDtypeStruct((1, LOCAL, 2, SIDE, SIDE), BF16),
-        in_specs=[pl.BlockSpec((SLOTS, 1, 2 * LOCAL, SIDE), lambda c: (0, c, 0, 0))],
-        out_specs=pl.BlockSpec((1, LOCAL, 2, SLOTS, SIDE), lambda c: (0, 0, 0, c, 0)),
+        out_shape=jax.ShapeDtypeStruct((1, LOCAL, 2, SLOTS, SIDE), BF16),
         scratch_shapes=[pltpu.VMEM((2 * LOCAL * SLOTS, SIDE), F32)],
         compiler_params=pltpu.CompilerParams(vmem_limit_bytes=24 * MIB),
+        cost_estimate=pl.CostEstimate(flops=0, bytes_accessed=8 * MIB, transcendentals=0),
         name="unpack",
     )(parcels)
 
 
-def correlate_kernel(g_ref, h_ref, w1_ref, w2_ref, w3_ref, w4_ref, out_ref, wide, mid, back, tail):
+def correlate_kernel(in_ref, w1_ref, w2_ref, w3_ref, w4_ref, out_ref, wide, mid, back, tail):
     chunk = 2 * LOCAL
 
     def fill(source, carry):
         start = pl.multiple_of(source * chunk, chunk)
-        wide[0, pl.ds(start, chunk), :] = g_ref[source, 0].astype(F32)
-        wide[1, pl.ds(start, chunk), :] = h_ref[source, 0].astype(F32)
+        for which in range(2):
+            block = in_ref[source, which].reshape(chunk, SIDE)
+            wide[which, pl.ds(start, chunk), :] = block.astype(F32)
         return carry
 
     def first(n, carry):
@@ -197,76 +207,96 @@
     def emit(slot, carry):
         for part in range(2):
             line = tail[pl.ds(part * SLOTS + slot, LOCAL, stride=OUTER), :]
-            out_ref[slot, 0, part * LOCAL : (part + 1) * LOCAL, :] = line.astype(BF16)
+            out_ref[slot, part * LOCAL : (part + 1) * LOCAL, :] = line.astype(BF16)
         return carry
 
     lax.fori_loop(0, SLOTS, fill, 0, unroll=4)
-    lax.fori_loop(0, LOCAL, first, 0, unroll=2)
-    lax.fori_loop(0, OUTER, middle, 0, unroll=4)
-    lax.fori_loop(0, LOCAL // 2, last, 0, unroll=2)
-    lax.fori_loop(0, SLOTS, emit, 0, unroll=4)
-
-
-def correlate(less, greater, tables):
-    parcel = pl.BlockSpec((SLOTS, 1, 2 * LOCAL, SIDE), lambda c: (0, c, 0, 0))
-    whole = [
-        pl.BlockSpec(t.shape, lambda c, rank=t.ndim: (0,) * rank, pipeline_mode=pl.Buffered(1))
-        for t in tables
-    ]
+    lax.fori_loop(0, LOCAL, first, 0, unroll=U1)
+    lax.fori_loop(0, OUTER, middle, 0, unroll=U2)
+    lax.fori_loop(0, LOCAL // 2, last, 0, unroll=U4)
+    lax.fori_loop(0, SLOTS, emit, 0, unroll=8)
+
+
+U1, U2, U4 = 8, 32, 8
+
+
+def correlate(parcels, tables):
     return pl.pallas_call(
         correlate_kernel,
-        grid=(HALF,),
-        out_shape=jax.ShapeDtypeStruct((SLOTS, HALF, 2 * LOCAL, SIDE), BF16),
-        in_specs=[parcel, parcel, *whole],
-        out_specs=parcel,
+        out_shape=jax.ShapeDtypeStruct((SLOTS, 2 * LOCAL, SIDE), BF16),
         scratch_shapes=[
             pltpu.VMEM((2, ENERGIES * 2, SIDE), F32),
             pltpu.VMEM((2, LOCAL * 2 * OUTER, SIDE), F32),
             pltpu.VMEM((OUTER * 2 * LOCAL, SIDE), F32),
             pltpu.VMEM((LOCAL * OUTER, SIDE), F32),
         ],
-        compiler_params=pltpu.CompilerParams(vmem_limit_bytes=52 * MIB),
+        compiler_params=pltpu.CompilerParams(vmem_limit_bytes=60 * MIB),
+        cost_estimate=pl.CostEstimate(
+            flops=12 * 10**9, bytes_accessed=40 * MIB, transcendentals=0
+        ),
         name="correlate",
-    )(less, greater, *tables)
+    )(parcels, *tables)
 
 
 SPAN = 8
-
-
-def screen_kernel(lower_ref, own_ref, upper_ref, left_ref, right_ref, out_ref):
-    def step(n, carry):
-        fields = []
-        for which, ref in enumerate((lower_ref, own_ref, upper_ref)):
-            both = jnp.concatenate([ref[0, n, 0], ref[0, n, 1]], axis=1)
-            fields.append(mm(left_ref[which], both).astype(BF16))
-        for part in range(2):
-            cols = slice(part * SIDE, (part + 1) * SIDE)
-            row = jnp.concatenate([field[:, cols] for field in fields], axis=1)
-            result = mm(row, right_ref[...]).astype(BF16)
-            out_ref[0, n, part] = result[:, :SIDE]
-            out_ref[0, n, 2 + part] = result[:, SIDE:]
-        return carry
-
-    lax.fori_loop(0, SPAN, step, 0, unroll=2)
-
-
-def screen(lower, own, upper, left, right):
-    field = pl.BlockSpec((1, SPAN, 2, SIDE, SIDE), lambda s: (0, s, 0, 0, 0))
+GROUP = 4
+
+
+def screen_kernel(*refs):
+    left_ref, right_ref, out_ref, polar_ref = refs[6:]
+
+    def step(group, carry):
+        rows = []
+        for inner in range(GROUP):
+            n = group * GROUP + inner
+            fields = []
+            for which in range(3):
+                top, bottom = refs[2 * which : 2 * which + 2]
+                blocks = [
+                    jnp.concatenate([top[0, n, part], bottom[0, n, part]], axis=0)
+                    for part in range(2)
+                ]
+                if which == 1:
+                    polar_ref[0, n, 0] = blocks[0]
+                    polar_ref[0, n, 1] = blocks[1]
+                both = jnp.concatenate(blocks, axis=1)
+                fields.append(mm(left_ref[which], both).astype(BF16))
+            for part in range(2):
+                cols = slice(part * SIDE, (part + 1) * SIDE)
+                rows.append(jnp.concatenate([field[:, cols] for field in fields], axis=1))
+        result = mm(jnp.concatenate(rows, axis=0), right_ref[...]).astype(BF16)
+        for inner in range(GROUP):
+            for part in range(2):
+                start = (2 * inner + part) * SIDE
+                block = result[start : start + SIDE]
+                out_ref[0, group * GROUP + inner, part] = block[:, :SIDE]
+                out_ref[0, group * GROUP + inner, 2 + part] = block[:, SIDE:]
+        return carry
+
+    lax.fori_loop(0, SPAN // GROUP, step, 0, unroll=True)
+
+
+def screen(one, own, two, left, right):
+    field = pl.BlockSpec((1, SPAN, 2, SLOTS, SIDE), lambda s: (0, s, 0, 0, 0))
     return pl.pallas_call(
         screen_kernel,
         grid=(LOCAL // SPAN,),
-        out_shape=jax.ShapeDtypeStruct((1, LOCAL, 4, SIDE, SIDE), BF16),
-        in_specs=[
-            field,
-            field,
-            field,
+        out_shape=[
+            jax.ShapeDtypeStruct((1, LOCAL, 4, SIDE, SIDE), BF16),
+            jax.ShapeDtypeStruct((1, LOCAL, 2, SIDE, SIDE), BF16),
+        ],
+        in_specs=[field] * 6
+        + [
             pl.BlockSpec(left.shape, lambda s: (0, 0, 0)),
             pl.BlockSpec(right.shape, lambda s: (0, 0)),
         ],
-        out_specs=pl.BlockSpec((1, SPAN, 4, SIDE, SIDE), lambda s: (0, s, 0, 0, 0)),
-        compiler_params=pltpu.CompilerParams(vmem_limit_bytes=32 * MIB),
+        out_specs=[
+            pl.BlockSpec((1, SPAN, 4, SIDE, SIDE), lambda s: (0, s, 0, 0, 0)),
+            pl.BlockSpec((1, SPAN, 2, SIDE, SIDE), lambda s: (0, s, 0, 0, 0)),
+        ],
+        compiler_params=pltpu.CompilerParams(vmem_limit_bytes=60 * MIB),
         name="screen",
-    )(lower, own, upper, left, right)
+    )(*one, *own, *two, left, right)
 
 
 def from_below(cells):
@@ -277,6 +307,12 @@
 def from_above(cells):
     ends = lax.axis_size("len") - 1
     return lax.ppermute(cells, "len", [(i + 1, i) for i in range(ends)])
+
+
+def swap(cells, first):
+    ends = lax.axis_size("len") - 1
+    pairs = [(i, i + 1) for i in range(first, ends, 2)]
+    return lax.ppermute(cells, "len", pairs + [(j, i) for i, j in pairs])
 
 
 def exchange(parcels):
@@ -287,25 +323,31 @@
     own_diag, own_up = coulomb[0, 0], coulomb[0, 1]
     prev_up = from_below(coulomb[:, 1])[0]
     next_diag = from_above(coulomb[:, 0])[0]
-    left = jnp.stack([prev_up.T, own_diag, own_up])
-    right = jnp.concatenate(
-        [
-            jnp.concatenate([prev_up, jnp.zeros_like(prev_up)], axis=1),
-            jnp.concatenate([own_diag, own_up], axis=1),
-            jnp.concatenate([own_up.T, next_diag], axis=1),
-        ],
-        axis=0,
-    )
+    below = (prev_up.T, jnp.concatenate([prev_up, jnp.zeros_like(prev_up)], axis=1))
+    above = (own_up, jnp.concatenate([own_up.T, next_diag], axis=1))
+    odd = lax.axis_index("len") % 2 == 1
+    one, two = [
+        [jnp.where(odd, x, y) for x, y in zip(*order)]
+        for order in ((below, above), (above, below))
+    ]
+    left = jnp.stack([one[0], own_diag, two[0]])
+    middle = jnp.concatenate([own_diag, own_up], axis=1)
+    right = jnp.concatenate([one[1], middle, two[1]], axis=0)
     return left, right
 
 
 def body(less_green, greater_green, coulomb):
-    left, right = coefficients(coulomb)
     tables = [jnp.asarray(table) for table in TABLES]
-    less = exchange(pack(less_green))
-    greater = exchange(pack(greater_green))
-    polar = unpack(exchange(correlate(less, greater, tables)))
-    screened = screen(from_below(polar), polar, from_above(polar), left, right)
+    packed = [pack(less_green, greater_green, 0)]
+    later = lax.optimization_barrier((less_green, greater_green, *coefficients(coulomb)))
+    left, right = later[2:]
+    packed.append(pack(later[0], later[1], 1))
+    arrived = [exchange(parcels) for parcels in packed]
+    returned = [exchange(correlate(parcels, tables)) for parcels in arrived]
+    own = [unpack(parcels) for parcels in returned]
+    one = [swap(rows, 0) for rows in own]
+    two = [swap(rows, 1) for rows in own]
+    screened, polar = screen(one, own, two, left, right)
     return polar, screened
 
 

time: 296 us -> 224 us (0.76)
  blocking collectives: 110 us -> 0 us
  starting transfers between devices: 28.9 us -> 65.5 us
  waiting for transfers between devices: 62 us -> 85 us
  Pallas kernels: 87.9 us -> 68.9 us
  local copies, waits for them, and re-layouts: 5.02 us -> 1.24 us
    all_to_all x2 -> x0, blocking collectives: 110 us -> none  [exchange(): lax.all_to_all(parcels, 'eng', split_axis=0, concat_axis=0, tiled=True)]
    all_to_all x1 -> x4, starting transfers between devices: 13.8 us -> 40.4 us  [exchange(): lax.all_to_all(parcels, 'eng', split_axis=0, concat_axis=0, tiled=True)]
    all_to_all x1 -> x4, waiting for transfers between devices: 43.1 us -> 68.5 us  [exchange(): lax.all_to_all(parcels, 'eng', split_axis=0, concat_axis=0, tiled=True)]
    pallas_call x5 -> x7, Pallas kernels: 87.9 us -> 68.9 us  [the longest x2 46.6 us: correlate(): pl.pallas_call(correlate_kernel, out_shape=jax.ShapeDtypeStruct((SLOTS, 2...]
    ppermute x2 -> x1, waiting for transfers between devices: 18.9 us -> 0.01 us  [from_below(): return lax.ppermute(cells, 'len', [(i, i + 1) for i in range(ends)])]
    ppermute x0 -> x4, starting transfers between devices: none -> 17.8 us  [swap(): return lax.ppermute(cells, 'len', pairs + [(j, i) for i, j in pairs])]
    ppermute x0 -> x4, waiting for transfers between devices: none -> 12.4 us  [swap(): return lax.ppermute(cells, 'len', pairs + [(j, i) for i, j in pairs])]
    ppermute x2 -> x1, starting transfers between devices: 8.2 us -> 1.92 us  [from_above(): return lax.ppermute(cells, 'len', [(i + 1, i) for i in range(ends)])]
  transfers between devices with their start and end apart: 5 -> 10, of which waited for: 2 -> 6; matrix products, arithmetic and copies ran while one was open for 0% -> 1% of each run, Pallas kernels for 1% -> 25%
where the time goes in v2:
time: 224 us; the launch traced here: 223 us
  waiting for transfers between devices  85 us (38%)
  Pallas kernels  68.9 us (31%)
  starting transfers between devices  65.5 us (29%)
    all_to_all x4, waiting for transfers between devices, exchange(): lax.all_to_all(parcels, 'eng', split_axis=0, concat_axis=0, tiled=True)  68.5 us
    pallas_call x2, Pallas kernels, correlate(): pl.pallas_call(correlate_kernel, out_shape=jax.ShapeDtypeStruct((SLOTS, 2...  46.6 us
    all_to_all x4, starting transfers between devices, exchange(): lax.all_to_all(parcels, 'eng', split_axis=0, concat_axis=0, tiled=True)  40.4 us
    ppermute x4, starting transfers between devices, swap(): return lax.ppermute(cells, 'len', pairs + [(j, i) for i, j in pairs])  17.8 us
    ppermute x4, waiting for transfers between devices, swap(): return lax.ppermute(cells, 'len', pairs + [(j, i) for i, j in pairs])  12.4 us
    pallas_call x2, Pallas kernels, pack(): pl.pallas_call(pack_kernel, grid=(steps,), out_shape=jax.ShapeDtypeStruct...  10.3 us
    pallas_call x1, Pallas kernels, screen(): pl.pallas_call(screen_kernel, grid=(LOCAL // SPAN,), out_shape=[jax.Shape...  8.03 us
    ppermute x1, starting transfers between devices, from_below(): return lax.ppermute(cells, 'len', [(i, i + 1) for i in range(ends)])  5.37 us
  transfers between devices with their start and end apart: 10, of which 6 were waited for; matrix products, arithmetic and copies ran while one was open for 1% of the time, Pallas kernels for 25%

profile of v2, /device:TPU:1, one launch (start us, length us, event | category | flops | bytes accessed | tf_op | source)
XLA Modules:
  0.0 222.9 jit_solution(10261723232724673164)
XLA Ops:
  0.6 5.1 %pack.2 = bf16[64,2,2,32,128]{4,3,2,1,0:T(8,128)(2,1)} custom-call(bf16[1,32,2,128,128]{4,3,2,1,0:T(8,128)(2,1)} %less_ref.2, bf16[1,32,2,128,128]{4,3,2,1,0:T(8,128)(2,1)} %greater_ref.2), custom_call_target="tpu_custom_call" | custom-call | bytes 8388608 | tf_op jit(solution)/shard_map/pack/pallas_call | solution.py:99
  5.8 13.6 %all-to-all-start = ((bf16[64,2,2,32,128]{4,3,2,1,0:T(8,128)(2,1)}), bf16[64,2,2,32,128]{4,3,2,1,0:T(8,128)(2,1)S(1)}, u32[]{:S(2)}, u32[]{:S(2)}) async-start(bf16[64,2,2,32,128]{4,3,2,1,0:T(8,128)(2,1)} %pack.2), calls=%async_computation | async-start | bytes 4194304 | tf_op jit(solution)/shard_map/all_to_all | solution.py:319
  19.5 5.4 %collective-permute-start.1 = (bf16[1,128,128]{2,1,0:T(8,128)(2,1)S(1)}, bf16[1,128,128]{2,1,0:T(8,128)(2,1)S(1)}, u32[]{:S(2)}, u32[]{:S(2)}) collective-permute-start(bf16[1,128,128]{2,1,0:T(8,128)(2,1)S(1)} %get-tuple-element.22), channel_id=1, source_target_pairs={{0,64},{64,128},{128,192},{1,65},{65,129},{129,193},{2,66},{66,130... | collective-permute-start | bytes 98312 | tf_op jit(solution)/shard_map/ppermute | solution.py:304
  24.8 1.9 collective-permute-start.2
  27.0 0.7 pad_maximum_fusion.1.refs_6_
  27.7 4.2 %collective-permute-done.2 = bf16[1,128,128]{2,1,0:T(8,128)(2,1)S(1)} collective-permute-done((bf16[1,128,128]{2,1,0:T(8,128)(2,1)S(1)}, bf16[1,128,128]{2,1,0:T(8,128)(2,1)S(1)}, u32[]{:S(2)}, u32[]{:S(2)}) %collective-permute-start.2) | collective-permute-done | bytes 32800 | tf_op jit(solution)/shard_map/ppermute | solution.py:309
  31.9 0.7 pad_maximum_fusion.refs_7_
  32.6 5.1 %pack.3 = bf16[64,2,2,32,128]{4,3,2,1,0:T(8,128)(2,1)} custom-call(bf16[1,32,2,128,128]{4,3,2,1,0:T(8,128)(2,1)} %less_ref.2, bf16[1,32,2,128,128]{4,3,2,1,0:T(8,128)(2,1)} %greater_ref.2), custom_call_target="tpu_custom_call" | custom-call | bytes 8388608 | tf_op jit(solution)/shard_map/pack/pallas_call | solution.py:99
  37.7 30.1 %all-to-all-done.in_ref = bf16[64,2,2,32,128]{4,3,2,1,0:T(8,128)(2,1)S(1)} async-done(((bf16[64,2,2,32,128]{4,3,2,1,0:T(8,128)(2,1)}), bf16[64,2,2,32,128]{4,3,2,1,0:T(8,128)(2,1)S(1)}, u32[]{:S(2)}, u32[]{:S(2)}) %all-to-all-start) | async-done | bytes 2097184 | tf_op jit(solution)/shard_map/all_to_all | solution.py:319
  67.9 7.9 %all-to-all-start.2 = ((bf16[64,2,2,32,128]{4,3,2,1,0:T(8,128)(2,1)}), bf16[64,2,2,32,128]{4,3,2,1,0:T(8,128)(2,1)}, u32[]{:S(2)}, u32[]{:S(2)}) async-start(bf16[64,2,2,32,128]{4,3,2,1,0:T(8,128)(2,1)} %pack.3), calls=%async_computation.2 | async-start | bytes 4194304 | tf_op jit(solution)/shard_map/all_to_all | solution.py:319
  75.8 23.3 %correlate.2 = bf16[64,64,128]{2,1,0:T(8,128)(2,1)} custom-call(bf16[64,2,2,32,128]{4,3,2,1,0:T(8,128)(2,1)} %copy-done.2, bf16[256,256]{1,0:T(8,128)(2,1)} %constant.30.clone.w1_ref, bf16[128,64,192]{2,1,0:T(8,128)(2,1)} %constant.31.clone.w2_ref, bf16[128,64,192]{2,1,0:T(8,128)(2,1)} %constant.32.clone.w3_ref, bf16[256,256]{1,0:T(8,128)(2,1)} %constant.33.clone.w4_ref), custom_call_target="tpu_custom_call" | custom-call | flops 12000000000 | bytes 41943040 | tf_op jit(solution)/shard_map/correlate/pallas_call | solution.py:224
  99.1 23.5 %all-to-all-done.2.in_ref = bf16[64,2,2,32,128]{4,3,2,1,0:T(8,128)(2,1)} async-done(((bf16[64,2,2,32,128]{4,3,2,1,0:T(8,128)(2,1)}), bf16[64,2,2,32,128]{4,3,2,1,0:T(8,128)(2,1)}, u32[]{:S(2)}, u32[]{:S(2)}) %all-to-all-start.2) | async-done | bytes 2097184 | tf_op jit(solution)/shard_map/all_to_all | solution.py:319
  122.6 9.2 %all-to-all-start.1 = ((bf16[64,64,128]{2,1,0:T(8,128)(2,1)}), bf16[64,64,128]{2,1,0:T(8,128)(2,1)S(1)}, u32[]{:S(2)}, u32[]{:S(2)}) async-start(bf16[64,64,128]{2,1,0:T(8,128)(2,1)} %correlate.2), calls=%async_computation.1 | async-start | bytes 2097152 | tf_op jit(solution)/shard_map/all_to_all | solution.py:319
  131.8 23.3 %correlate.3 = bf16[64,64,128]{2,1,0:T(8,128)(2,1)} custom-call(bf16[64,2,2,32,128]{4,3,2,1,0:T(8,128)(2,1)} %all-to-all-done.2.in_ref, bf16[256,256]{1,0:T(8,128)(2,1)} %constant.30.clone.w1_ref, bf16[128,64,192]{2,1,0:T(8,128)(2,1)} %constant.31.clone.w2_ref, bf16[128,64,192]{2,1,0:T(8,128)(2,1)} %constant.32.clone.w3_ref, ...), custom_call_target="tpu_custom_call" | custom-call | flops 12000000000 | bytes 41943040 | tf_op jit(solution)/shard_map/correlate/pallas_call | solution.py:224
  155.1 0.8 all-to-all-done.1.in_ref
  155.9 9.7 %all-to-all-start.3 = ((bf16[64,64,128]{2,1,0:T(8,128)(2,1)}), bf16[64,64,128]{2,1,0:T(8,128)(2,1)S(1)}, u32[]{:S(2)}, u32[]{:S(2)}) async-start(bf16[64,64,128]{2,1,0:T(8,128)(2,1)} %correlate.3), calls=%async_computation.3 | async-start | bytes 2097152 | tf_op jit(solution)/shard_map/all_to_all | solution.py:319
  165.6 2.0 unpack.2.refs_2_
  167.5 7.2 %collective-permute-start.4 = (bf16[1,32,2,64,128]{4,3,2,1,0:T(8,128)(2,1)S(1)}, bf16[1,32,2,64,128]{4,3,2,1,0:T(8,128)(2,1)}, u32[]{:S(2)}, u32[]{:S(2)}) collective-permute-start(bf16[1,32,2,64,128]{4,3,2,1,0:T(8,128)(2,1)S(1)} %unpack.2.refs_2_), channel_id=1, source_target_pairs={{64,128},{128,64},{65,129},{129,65},{66,130},{130,66},{67,131},{13... | collective-permute-start | bytes 3145736 | tf_op jit(solution)/shard_map/ppermute | solution.py:315
  174.9 14.1 %all-to-all-done.3.in_ref = bf16[64,64,128]{2,1,0:T(8,128)(2,1)S(1)} async-done(((bf16[64,64,128]{2,1,0:T(8,128)(2,1)}), bf16[64,64,128]{2,1,0:T(8,128)(2,1)S(1)}, u32[]{:S(2)}, u32[]{:S(2)}) %all-to-all-start.3) | async-done | bytes 1048608 | tf_op jit(solution)/shard_map/all_to_all | solution.py:319
  189.0 2.0 unpack.3.refs_3_
  190.9 10.4 %collective-permute-start.5 = (bf16[1,32,2,64,128]{4,3,2,1,0:T(8,128)(2,1)S(1)}, bf16[1,32,2,64,128]{4,3,2,1,0:T(8,128)(2,1)S(1)}, u32[]{:S(2)}, u32[]{:S(2)}) collective-permute-start(bf16[1,32,2,64,128]{4,3,2,1,0:T(8,128)(2,1)S(1)} %unpack.3.refs_3_), channel_id=1, source_target_pairs={{64,128},{128,64},{65,129},{129,65},{66,130},{130,66},{67,131},{13... | collective-permute-start | bytes 3145736 | tf_op jit(solution)/shard_map/ppermute | solution.py:315
  201.5 12.3 %collective-permute-done.5.refs_5_ = bf16[1,32,2,64,128]{4,3,2,1,0:T(8,128)(2,1)S(1)} collective-permute-done((bf16[1,32,2,64,128]{4,3,2,1,0:T(8,128)(2,1)S(1)}, bf16[1,32,2,64,128]{4,3,2,1,0:T(8,128)(2,1)S(1)}, u32[]{:S(2)}, u32[]{:S(2)}) %collective-permute-start.5) | collective-permute-done | bytes 1048608 | tf_op jit(solution)/shard_map/ppermute | solution.py:315
  213.9 1.0 copy-done.3
  214.8 8.0 %screen.1 = (bf16[1,32,4,128,128]{4,3,2,1,0:T(8,128)(2,1)}, bf16[1,32,2,128,128]{4,3,2,1,0:T(8,128)(2,1)}) custom-call(bf16[1,32,2,64,128]{4,3,2,1,0:T(8,128)(2,1)} %collective-permute-done.refs_0_, bf16[1,32,2,64,128]{4,3,2,1,0:T(8,128)(2,1)} %collective-permute-done.3.refs_1_, bf16[1,32,2,64,128]{4,3,2,1,0:T(8,128)(2,1)} %copy-done, ...), custom_call_target="tpu_custom_call" | custom-call | tf_op jit(solution)/shard_map/screen/pallas_call | solution.py:281
  (20 shorter events, 0.5 us)
Async XLA Ops:
  5.8 13.6 %copy-start.4 = (bf16[1,2,128,128]{3,2,1,0:T(8,128)(2,1)S(1)}, bf16[1,2,128,128]{3,2,1,0:T(8,128)(2,1)}, u32[]{:S(2)}) copy-start(bf16[1,2,128,128]{3,2,1,0:T(8,128)(2,1)} %param.9) | copy-start | bytes 196612
  5.8 62.1 %all-to-all-start = ((bf16[64,2,2,32,128]{4,3,2,1,0:T(8,128)(2,1)}), bf16[64,2,2,32,128]{4,3,2,1,0:T(8,128)(2,1)S(1)}, u32[]{:S(2)}, u32[]{:S(2)}) async-start(bf16[64,2,2,32,128]{4,3,2,1,0:T(8,128)(2,1)} %pack.2), calls=%async_computation | async-start | bytes 4194304 | tf_op jit(solution)/shard_map/all_to_all | solution.py:319
  19.5 7.4 %collective-permute-start.1 = (bf16[1,128,128]{2,1,0:T(8,128)(2,1)S(1)}, bf16[1,128,128]{2,1,0:T(8,128)(2,1)S(1)}, u32[]{:S(2)}, u32[]{:S(2)}) collective-permute-start(bf16[1,128,128]{2,1,0:T(8,128)(2,1)S(1)} %get-tuple-element.22), channel_id=1, source_target_pairs={{0,64},{64,128},{128,192},{1,65},{65,129},{129,193},{2,66},{66,130... | collective-permute-start | bytes 98312 | tf_op jit(solution)/shard_map/ppermute | solution.py:304
  24.8 7.0 %collective-permute-start.2 = (bf16[1,128,128]{2,1,0:T(8,128)(2,1)S(1)}, bf16[1,128,128]{2,1,0:T(8,128)(2,1)S(1)}, u32[]{:S(2)}, u32[]{:S(2)}) collective-permute-start(bf16[1,128,128]{2,1,0:T(8,128)(2,1)S(1)} %get-tuple-element.21), channel_id=1, source_target_pairs={{64,0},{128,64},{192,128},{65,1},{129,65},{193,129},{66,2},{130,66... | collective-permute-start | bytes 98312 | tf_op jit(solution)/shard_map/ppermute | solution.py:309
  67.8 7.9 %copy-start.2 = (bf16[64,2,2,32,128]{4,3,2,1,0:T(8,128)(2,1)}, bf16[64,2,2,32,128]{4,3,2,1,0:T(8,128)(2,1)S(1)}, u32[]{:S(2)}) copy-start(bf16[64,2,2,32,128]{4,3,2,1,0:T(8,128)(2,1)S(1)} %all-to-all-done.in_ref) | copy-start | bytes 6291460
  67.9 54.7 %all-to-all-start.2 = ((bf16[64,2,2,32,128]{4,3,2,1,0:T(8,128)(2,1)}), bf16[64,2,2,32,128]{4,3,2,1,0:T(8,128)(2,1)}, u32[]{:S(2)}, u32[]{:S(2)}) async-start(bf16[64,2,2,32,128]{4,3,2,1,0:T(8,128)(2,1)} %pack.3), calls=%async_computation.2 | async-start | bytes 4194304 | tf_op jit(solution)/shard_map/all_to_all | solution.py:319
  122.6 33.3 %all-to-all-start.1 = ((bf16[64,64,128]{2,1,0:T(8,128)(2,1)}), bf16[64,64,128]{2,1,0:T(8,128)(2,1)S(1)}, u32[]{:S(2)}, u32[]{:S(2)}) async-start(bf16[64,64,128]{2,1,0:T(8,128)(2,1)} %correlate.2), calls=%async_computation.1 | async-start | bytes 2097152 | tf_op jit(solution)/shard_map/all_to_all | solution.py:319
  155.9 33.1 %all-to-all-start.3 = ((bf16[64,64,128]{2,1,0:T(8,128)(2,1)}), bf16[64,64,128]{2,1,0:T(8,128)(2,1)S(1)}, u32[]{:S(2)}, u32[]{:S(2)}) async-start(bf16[64,64,128]{2,1,0:T(8,128)(2,1)} %correlate.3), calls=%async_computation.3 | async-start | bytes 2097152 | tf_op jit(solution)/shard_map/all_to_all | solution.py:319
  167.5 46.3 %copy-start = (bf16[1,32,2,64,128]{4,3,2,1,0:T(8,128)(2,1)}, bf16[1,32,2,64,128]{4,3,2,1,0:T(8,128)(2,1)S(1)}, u32[]{:S(2)}) copy-start(bf16[1,32,2,64,128]{4,3,2,1,0:T(8,128)(2,1)S(1)} %unpack.2.refs_2_) | copy-start | bytes 3145732
  167.5 33.9 %collective-permute-start.4 = (bf16[1,32,2,64,128]{4,3,2,1,0:T(8,128)(2,1)S(1)}, bf16[1,32,2,64,128]{4,3,2,1,0:T(8,128)(2,1)}, u32[]{:S(2)}, u32[]{:S(2)}) collective-permute-start(bf16[1,32,2,64,128]{4,3,2,1,0:T(8,128)(2,1)S(1)} %unpack.2.refs_2_), channel_id=1, source_target_pairs={{64,128},{128,64},{65,129},{129,65},{66,130},{130,66},{67,131},{13... | collective-permute-start | bytes 3145736 | tf_op jit(solution)/shard_map/ppermute | solution.py:315
  174.8 26.7 %collective-permute-start = (bf16[1,32,2,64,128]{4,3,2,1,0:T(8,128)(2,1)S(1)}, bf16[1,32,2,64,128]{4,3,2,1,0:T(8,128)(2,1)}, u32[]{:S(2)}, u32[]{:S(2)}) collective-permute-start(bf16[1,32,2,64,128]{4,3,2,1,0:T(8,128)(2,1)S(1)} %unpack.2.refs_2_), channel_id=1, source_target_pairs={{0,64},{128,192},{64,0},{192,128},{1,65},{129,193},{65,1},{193,129... | collective-permute-start | bytes 3145736 | tf_op jit(solution)/shard_map/ppermute | solution.py:315
  190.9 22.9 %copy-start.1 = (bf16[1,32,2,64,128]{4,3,2,1,0:T(8,128)(2,1)}, bf16[1,32,2,64,128]{4,3,2,1,0:T(8,128)(2,1)S(1)}, u32[]{:S(2)}) copy-start(bf16[1,32,2,64,128]{4,3,2,1,0:T(8,128)(2,1)S(1)} %unpack.3.refs_3_) | copy-start | bytes 3145732
  190.9 22.9 %collective-permute-start.5 = (bf16[1,32,2,64,128]{4,3,2,1,0:T(8,128)(2,1)S(1)}, bf16[1,32,2,64,128]{4,3,2,1,0:T(8,128)(2,1)S(1)}, u32[]{:S(2)}, u32[]{:S(2)}) collective-permute-start(bf16[1,32,2,64,128]{4,3,2,1,0:T(8,128)(2,1)S(1)} %unpack.3.refs_3_), channel_id=1, source_target_pairs={{64,128},{128,64},{65,129},{129,65},{66,130},{130,66},{67,131},{13... | collective-permute-start | bytes 3145736 | tf_op jit(solution)/shard_map/ppermute | solution.py:315
  201.4 12.5 %collective-permute-start.3 = (bf16[1,32,2,64,128]{4,3,2,1,0:T(8,128)(2,1)S(1)}, bf16[1,32,2,64,128]{4,3,2,1,0:T(8,128)(2,1)}, u32[]{:S(2)}, u32[]{:S(2)}) collective-permute-start(bf16[1,32,2,64,128]{4,3,2,1,0:T(8,128)(2,1)S(1)} %unpack.3.refs_3_), channel_id=1, source_target_pairs={{0,64},{128,192},{64,0},{192,128},{1,65},{129,193},{65,1},{193,129... | collective-permute-start | bytes 3145736 | tf_op jit(solution)/shard_map/ppermute | solution.py:315
  213.8 1.0 copy-start.3

commit v3 on v2

--- a/solution.py
+++ b/solution.py
@@ -70,18 +70,19 @@
     return jnp.dot(left, right, preferred_element_type=F32)
 
 
-def pack_kernel(less_ref, greater_ref, out_ref, wide):
-    count = less_ref.shape[1]
+def pack_kernel(*refs):
+    *in_refs, out_ref, wide = refs
+    count = in_refs[0].shape[1]
 
     def fill(n, carry):
-        for which, ref in enumerate((less_ref, greater_ref)):
+        for which, ref in enumerate(in_refs):
             for part in range(2):
                 start = pl.multiple_of(((which * 2 + part) * count + n) * SLOTS, SLOTS)
                 wide[pl.ds(start, SLOTS), :] = ref[0, n, part].astype(F32)
         return carry
 
     def emit(row, carry):
-        for which in range(2):
+        for which in range(len(in_refs)):
             for part in range(2):
                 start = (which * 2 + part) * count * SLOTS + row
                 line = wide[pl.ds(start, count, stride=SLOTS), :]
@@ -92,43 +93,58 @@
     lax.fori_loop(0, SLOTS, emit, 0, unroll=8)
 
 
-def pack(less, greater, chunk):
+def pack(fields, chunk):
     steps = 2
     count = LOCAL // steps
-    field = pl.BlockSpec((1, count, 2, SLOTS, SIDE), lambda s: (0, s, 0, chunk, 0))
+    total = len(fields)
+    block = pl.BlockSpec((1, count, 2, SLOTS, SIDE), lambda s: (0, s, 0, chunk, 0))
     return pl.pallas_call(
         pack_kernel,
         grid=(steps,),
-        out_shape=jax.ShapeDtypeStruct((SLOTS, 2, 2, LOCAL, SIDE), BF16),
-        in_specs=[field, field],
-        out_specs=pl.BlockSpec((SLOTS, 2, 2, count, SIDE), lambda s: (0, 0, 0, s, 0)),
-        scratch_shapes=[pltpu.VMEM((4 * count * SLOTS, SIDE), F32)],
+        out_shape=jax.ShapeDtypeStruct((SLOTS, total, 2, LOCAL, SIDE), BF16),
+        in_specs=[block] * total,
+        out_specs=pl.BlockSpec((SLOTS, total, 2, count, SIDE), lambda s: (0, 0, 0, s, 0)),
+        scratch_shapes=[pltpu.VMEM((2 * total * count * SLOTS, SIDE), F32)],
         compiler_params=pltpu.CompilerParams(vmem_limit_bytes=60 * MIB),
-        cost_estimate=pl.CostEstimate(flops=0, bytes_accessed=8 * MIB, transcendentals=0),
+        cost_estimate=pl.CostEstimate(
+            flops=0, bytes_accessed=4 * total * MIB, transcendentals=0
+        ),
         name="pack",
-    )(less, greater)
-
-
-def unpack_kernel(in_ref, out_ref, wide):
+    )(*fields)
+
+
+def unpack_kernel(in_ref, out_ref, *rest):
+    *half_refs, wide = rest
+
     def fill(row, carry):
         start = pl.multiple_of(row * 2 * LOCAL, 2 * LOCAL)
         wide[pl.ds(start, 2 * LOCAL), :] = in_ref[row].astype(F32)
         return carry
 
-    def emit(n, carry):
-        for part in range(2):
-            line = wide[pl.ds(part * LOCAL + n, SLOTS, stride=2 * LOCAL), :]
-            out_ref[0, n, part] = line.astype(BF16)
-        return carry
+    def emit_from(begin, half_ref):
+        def emit(step, carry):
+            n = begin + step
+            for part in range(2):
+                line = wide[pl.ds(part * LOCAL + n, SLOTS, stride=2 * LOCAL), :].astype(BF16)
+                out_ref[0, n, part] = line
+                if half_ref is not None:
+                    half_ref[0, step, part] = line
+            return carry
+
+        return emit
 
     lax.fori_loop(0, SLOTS, fill, 0, unroll=4)
-    lax.fori_loop(0, LOCAL, emit, 0, unroll=4)
-
-
-def unpack(parcels):
+    half = LOCAL // 2
+    for begin, half_ref in zip((0, half), half_refs or (None, None)):
+        lax.fori_loop(0, half, emit_from(begin, half_ref), 0, unroll=4)
+
+
+def unpack(parcels, in_halves):
+    shape = jax.ShapeDtypeStruct((1, LOCAL, 2, SLOTS, SIDE), BF16)
+    half = jax.ShapeDtypeStruct((1, LOCAL // 2, 2, SLOTS, SIDE), BF16)
     return pl.pallas_call(
         unpack_kernel,
-        out_shape=jax.ShapeDtypeStruct((1, LOCAL, 2, SLOTS, SIDE), BF16),
+        out_shape=[shape, half, half] if in_halves else [shape],
         scratch_shapes=[pltpu.VMEM((2 * LOCAL * SLOTS, SIDE), F32)],
         compiler_params=pltpu.CompilerParams(vmem_limit_bytes=24 * MIB),
         cost_estimate=pl.CostEstimate(flops=0, bytes_accessed=8 * MIB, transcendentals=0),
@@ -136,13 +152,22 @@
     )(parcels)
 
 
-def correlate_kernel(in_ref, w1_ref, w2_ref, w3_ref, w4_ref, out_ref, wide, mid, back, tail):
+def correlate_kernel(*refs):
+    in_refs, refs = refs[:-13], refs[-13:]
+    w1_ref, w2_from, w3_from, w4_ref, out_ref, wide, mid, back, tail, w2_ref, w3_ref = refs[:-2]
+    fetches = [
+        pltpu.make_async_copy(w2_from, w2_ref, refs[-2]),
+        pltpu.make_async_copy(w3_from, w3_ref, refs[-1]),
+    ]
+    for fetch in fetches:
+        fetch.start()
+    places = [(ref, inner) for ref in in_refs for inner in range(ref.shape[1])]
     chunk = 2 * LOCAL
 
     def fill(source, carry):
         start = pl.multiple_of(source * chunk, chunk)
-        for which in range(2):
-            block = in_ref[source, which].reshape(chunk, SIDE)
+        for which, (ref, inner) in enumerate(places):
+            block = ref[source, inner].reshape(chunk, SIDE)
             wide[which, pl.ds(start, chunk), :] = block.astype(F32)
         return carry
 
@@ -212,6 +237,8 @@
 
     lax.fori_loop(0, SLOTS, fill, 0, unroll=4)
     lax.fori_loop(0, LOCAL, first, 0, unroll=U1)
+    for fetch in fetches:
+        fetch.wait()
     lax.fori_loop(0, OUTER, middle, 0, unroll=U2)
     lax.fori_loop(0, LOCAL // 2, last, 0, unroll=U4)
     lax.fori_loop(0, SLOTS, emit, 0, unroll=8)
@@ -220,22 +247,28 @@
 U1, U2, U4 = 8, 32, 8
 
 
-def correlate(parcels, tables):
+def correlate(arrived, tables):
+    vmem = pl.BlockSpec(memory_space=pltpu.VMEM)
     return pl.pallas_call(
         correlate_kernel,
         out_shape=jax.ShapeDtypeStruct((SLOTS, 2 * LOCAL, SIDE), BF16),
+        in_specs=[vmem] * (len(arrived) + 1) + [pl.BlockSpec(memory_space=pl.ANY)] * 2 + [vmem],
         scratch_shapes=[
             pltpu.VMEM((2, ENERGIES * 2, SIDE), F32),
             pltpu.VMEM((2, LOCAL * 2 * OUTER, SIDE), F32),
             pltpu.VMEM((OUTER * 2 * LOCAL, SIDE), F32),
             pltpu.VMEM((LOCAL * OUTER, SIDE), F32),
+            pltpu.VMEM(tables[1].shape, BF16),
+            pltpu.VMEM(tables[2].shape, BF16),
+            pltpu.SemaphoreType.DMA,
+            pltpu.SemaphoreType.DMA,
         ],
         compiler_params=pltpu.CompilerParams(vmem_limit_bytes=60 * MIB),
         cost_estimate=pl.CostEstimate(
             flops=12 * 10**9, bytes_accessed=40 * MIB, transcendentals=0
         ),
         name="correlate",
-    )(parcels, *tables)
+    )(*arrived, *tables)
 
 
 SPAN = 8
@@ -243,7 +276,8 @@
 
 
 def screen_kernel(*refs):
-    left_ref, right_ref, out_ref, polar_ref = refs[6:]
+    left_ref, right_ref = refs[6:8]
+    out_ref, polar_ref = refs[-2:]
 
     def step(group, carry):
         rows = []
@@ -276,27 +310,37 @@
     lax.fori_loop(0, SPAN // GROUP, step, 0, unroll=True)
 
 
-def screen(one, own, two, left, right):
-    field = pl.BlockSpec((1, SPAN, 2, SLOTS, SIDE), lambda s: (0, s, 0, 0, 0))
+def screen(fields, left, right, half, results):
+    steps = LOCAL // (2 * SPAN)
+
+    def spec(parts):
+        return pl.BlockSpec((1, SPAN, parts, SIDE, SIDE), lambda s: (0, s + half * steps, 0, 0, 0))
+
+    def field_spec(field):
+        first = half * steps if field.shape[1] == LOCAL else 0
+        return pl.BlockSpec((1, SPAN, 2, SLOTS, SIDE), lambda s: (0, s + first, 0, 0, 0))
+
     return pl.pallas_call(
         screen_kernel,
-        grid=(LOCAL // SPAN,),
+        grid=(steps,),
         out_shape=[
             jax.ShapeDtypeStruct((1, LOCAL, 4, SIDE, SIDE), BF16),
             jax.ShapeDtypeStruct((1, LOCAL, 2, SIDE, SIDE), BF16),
         ],
-        in_specs=[field] * 6
+        in_specs=[field_spec(field) for field in fields]
         + [
             pl.BlockSpec(left.shape, lambda s: (0, 0, 0)),
             pl.BlockSpec(right.shape, lambda s: (0, 0)),
-        ],
-        out_specs=[
-            pl.BlockSpec((1, SPAN, 4, SIDE, SIDE), lambda s: (0, s, 0, 0, 0)),
-            pl.BlockSpec((1, SPAN, 2, SIDE, SIDE), lambda s: (0, s, 0, 0, 0)),
-        ],
-        compiler_params=pltpu.CompilerParams(vmem_limit_bytes=60 * MIB),
+        ]
+        + [pl.BlockSpec(memory_space=pl.ANY)] * len(results),
+        out_specs=[spec(4), spec(2)],
+        input_output_aliases={8 + i: i for i in range(len(results))},
+        compiler_params=pltpu.CompilerParams(vmem_limit_bytes=63 * MIB),
+        cost_estimate=pl.CostEstimate(
+            flops=2 * 10**9, bytes_accessed=10 * MIB, transcendentals=0
+        ),
         name="screen",
-    )(*one, *own, *two, left, right)
+    )(*fields, left, right, *results)
 
 
 def from_below(cells):
@@ -336,18 +380,32 @@
     return left, right
 
 
+def forward(less, greater, tables, groups):
+    arrived = [exchange(pack([(less, greater)[which] for which in group], 0)) for group in groups]
+    second = exchange(pack([less, greater], 1))
+    first = exchange(correlate(arrived, tables))
+    return first, correlate([second], tables)
+
+
 def body(less_green, greater_green, coulomb):
     tables = [jnp.asarray(table) for table in TABLES]
-    packed = [pack(less_green, greater_green, 0)]
-    later = lax.optimization_barrier((less_green, greater_green, *coefficients(coulomb)))
-    left, right = later[2:]
-    packed.append(pack(later[0], later[1], 1))
-    arrived = [exchange(parcels) for parcels in packed]
-    returned = [exchange(correlate(parcels, tables)) for parcels in arrived]
-    own = [unpack(parcels) for parcels in returned]
-    one = [swap(rows, 0) for rows in own]
-    two = [swap(rows, 1) for rows in own]
-    screened, polar = screen(one, own, two, left, right)
+    first, second = lax.cond(
+        lax.axis_index("len") % 2 == 0,
+        lambda x, y: forward(x, y, tables, ((0, 1),)),
+        lambda x, y: forward(x, y, tables, ((0,), (1,))),
+        less_green,
+        greater_green,
+    )
+    (top,) = unpack(first, False)
+    top, left, right = lax.optimization_barrier((top, *coefficients(coulomb)))
+    bottom, *halves = unpack(exchange(second), True)
+    one = [swap(top, 0), swap(bottom, 0)]
+    two = [swap(top, 1), *[swap(rows, 1) for rows in halves]]
+    results = ()
+    for half in range(2):
+        fields = (*one, top, bottom, two[0], two[1 + half])
+        results = screen(fields, left, right, half, results)
+    screened, polar = results
     return polar, screened
 
 

time: 224 us -> 206 us (0.920)
  waiting for transfers between devices: 85 us -> 72.5 us
  starting transfers between devices: 65.5 us -> 60.7 us
    ppermute x4 -> x5, waiting for transfers between devices: 12.4 us -> 4.9 us  [swap(): return lax.ppermute(cells, 'len', pairs + [(j, i) for i, j in pairs])]
    ppermute x4 -> x5, starting transfers between devices: 17.8 us -> 11.3 us  [swap(): return lax.ppermute(cells, 'len', pairs + [(j, i) for i, j in pairs])]
    pallas_call x2, Pallas kernels: 46.6 us -> 41.6 us  [correlate(): pl.pallas_call(correlate_kernel, out_shape=jax.ShapeDtypeStruct((SLOTS, 2...]
    all_to_all x4 -> x5, starting transfers between devices: 40.4 us -> 45.1 us  [exchange(): lax.all_to_all(parcels, 'eng', split_axis=0, concat_axis=0, tiled=True)]
    ppermute x1, waiting for transfers between devices: 4.17 us -> 0.59 us  [from_above(): return lax.ppermute(cells, 'len', [(i + 1, i) for i in range(ends)])]
    ppermute x1, starting transfers between devices: 5.37 us -> 1.92 us  [from_below(): return lax.ppermute(cells, 'len', [(i, i + 1) for i in range(ends)])]
    pallas_call x3 -> x4, Pallas kernels: 12 us -> 15.1 us  [the longest x2 9.9 us: screen(): pl.pallas_call(screen_kernel, grid=(steps,), out_shape=[jax.ShapeDtypeStr...]
    pallas_call x2 -> x3, Pallas kernels: 10.3 us -> 11.9 us  [pack(): pl.pallas_call(pack_kernel, grid=(steps,), out_shape=jax.ShapeDtypeStruct...]
  transfers between devices with their start and end apart: 10 -> 12, of which waited for: 6 -> 7; matrix products, arithmetic and copies ran while one was open for 1% -> 1% of each run, Pallas kernels for 25% -> 29%
where the time goes in v3:
time: 206 us; the launch traced here: 205 us
  waiting for transfers between devices  72.5 us (35%)
  Pallas kernels  68.5 us (33%)
  starting transfers between devices  60.7 us (29%)
    all_to_all x5, waiting for transfers between devices, exchange(): lax.all_to_all(parcels, 'eng', split_axis=0, concat_axis=0, tiled=True)  67.1 us
    all_to_all x5, starting transfers between devices, exchange(): lax.all_to_all(parcels, 'eng', split_axis=0, concat_axis=0, tiled=True)  45.1 us
    pallas_call x2, Pallas kernels, correlate(): pl.pallas_call(correlate_kernel, out_shape=jax.ShapeDtypeStruct((SLOTS, 2...  41.6 us
    pallas_call x3, Pallas kernels, pack(): pl.pallas_call(pack_kernel, grid=(steps,), out_shape=jax.ShapeDtypeStruct...  11.9 us
    ppermute x5, starting transfers between devices, swap(): return lax.ppermute(cells, 'len', pairs + [(j, i) for i, j in pairs])  11.3 us
    pallas_call x2, Pallas kernels, screen(): pl.pallas_call(screen_kernel, grid=(steps,), out_shape=[jax.ShapeDtypeStr...  9.9 us
    pallas_call x2, Pallas kernels, unpack(): pl.pallas_call(unpack_kernel, out_shape=[shape, half, half] if in_halves...  5.16 us
    ppermute x5, waiting for transfers between devices, swap(): return lax.ppermute(cells, 'len', pairs + [(j, i) for i, j in pairs])  4.9 us
  transfers between devices with their start and end apart: 12, of which 7 were waited for; matrix products, arithmetic and copies ran while one was open for 1% of the time, Pallas kernels for 29%

profile of v3, /device:TPU:1, one launch (start us, length us, event | category | flops | bytes accessed | tf_op | source)
XLA Modules:
  0.0 205.3 jit_solution(3300737270873373389)
XLA Ops:
  0.6 147.2 %conditional.1 = (bf16[64,64,128]{2,1,0:T(8,128)(2,1)}, bf16[64,64,128]{2,1,0:T(8,128)(2,1)}) conditional(s32[]{:T(128)} %convert_element_type.3, (bf16[1,32,2,128,128]{4,3,2,1,0:T(8,128)(2,1)}, bf16[1,32,2,128,128]{4,3,2,1,0:T(8,128)(2,1)}, bf16[256,256]{1,0:T(8,128)(2,1)}, bf16[128,64,192]{2,1,0:T(8,128)(2,1)}, bf16[128,64,192]{2,1,0:T(8,128)(2,1)}, ...), branch_computations={%region_0.1_spmd, %region_1.2_spmd} | conditional | flops 24000000000 | bytes 138412304 | solution.py:392
  0.7 3.3 %pack.5 = bf16[64,1,2,32,128]{4,3,2,1,0:T(8,128)(2,1)} custom-call(bf16[1,32,2,128,128]{4,3,2,1,0:T(8,128)(2,1)} %get-tuple-element.24.refs_0_), custom_call_target="tpu_custom_call" | custom-call | bytes 4194304 | tf_op jit(solution)/shard_map/cond/branch_0_fun/pack/pallas_call | solution.py:101
  4.0 13.5 %all-to-all-start = ((bf16[64,1,2,32,128]{4,3,2,1,0:T(8,128)(2,1)}), bf16[64,1,2,32,128]{4,3,2,1,0:T(8,128)(2,1)S(1)}, u32[]{:S(2)}, u32[]{:S(2)}) async-start(bf16[64,1,2,32,128]{4,3,2,1,0:T(8,128)(2,1)} %pack.5), calls=%async_computation | async-start | bytes 2097152 | tf_op jit(solution)/shard_map/cond/branch_0_fun/all_to_all | solution.py:363
  17.5 3.5 %pack.6 = bf16[64,1,2,32,128]{4,3,2,1,0:T(8,128)(2,1)} custom-call(bf16[1,32,2,128,128]{4,3,2,1,0:T(8,128)(2,1)} %get-tuple-element.25.refs_0_.refs_1_), custom_call_target="tpu_custom_call" | custom-call | bytes 4194304 | tf_op jit(solution)/shard_map/cond/branch_0_fun/pack/pallas_call | solution.py:101
  21.0 19.0 %all-to-all-done.refs_0_ = bf16[64,1,2,32,128]{4,3,2,1,0:T(8,128)(2,1)S(1)} async-done(((bf16[64,1,2,32,128]{4,3,2,1,0:T(8,128)(2,1)}), bf16[64,1,2,32,128]{4,3,2,1,0:T(8,128)(2,1)S(1)}, u32[]{:S(2)}, u32[]{:S(2)}) %all-to-all-start) | async-done | bytes 1048608 | tf_op jit(solution)/shard_map/cond/branch_0_fun/all_to_all | solution.py:363
  40.0 10.6 %all-to-all-start.1 = ((bf16[64,1,2,32,128]{4,3,2,1,0:T(8,128)(2,1)}), bf16[64,1,2,32,128]{4,3,2,1,0:T(8,128)(2,1)}, u32[]{:S(2)}, u32[]{:S(2)}) async-start(bf16[64,1,2,32,128]{4,3,2,1,0:T(8,128)(2,1)} %pack.6), calls=%async_computation.1 | async-start | bytes 2097152 | tf_op jit(solution)/shard_map/cond/branch_0_fun/all_to_all | solution.py:363
  50.6 5.0 %pack.7 = bf16[64,2,2,32,128]{4,3,2,1,0:T(8,128)(2,1)} custom-call(bf16[1,32,2,128,128]{4,3,2,1,0:T(8,128)(2,1)S(1)} %copy-done.2, bf16[1,32,2,128,128]{4,3,2,1,0:T(8,128)(2,1)} %get-tuple-element.25.refs_0_.refs_1_), custom_call_target="tpu_custom_call" | custom-call | bytes 8388608 | tf_op jit(solution)/shard_map/cond/branch_0_fun/pack/pallas_call | solution.py:101
  55.6 13.6 %all-to-all-done.1.refs_1_ = bf16[64,1,2,32,128]{4,3,2,1,0:T(8,128)(2,1)} async-done(((bf16[64,1,2,32,128]{4,3,2,1,0:T(8,128)(2,1)}), bf16[64,1,2,32,128]{4,3,2,1,0:T(8,128)(2,1)}, u32[]{:S(2)}, u32[]{:S(2)}) %all-to-all-start.1) | async-done | bytes 1048608 | tf_op jit(solution)/shard_map/cond/branch_0_fun/all_to_all | solution.py:363
  69.2 5.6 %all-to-all-start.3 = ((bf16[64,2,2,32,128]{4,3,2,1,0:T(8,128)(2,1)}), bf16[64,2,2,32,128]{4,3,2,1,0:T(8,128)(2,1)S(1)}, u32[]{:S(2)}, u32[]{:S(2)}) async-start(bf16[64,2,2,32,128]{4,3,2,1,0:T(8,128)(2,1)} %pack.7), calls=%async_computation.3 | async-start | bytes 4194304 | tf_op jit(solution)/shard_map/cond/branch_0_fun/all_to_all | solution.py:363
  74.8 20.8 %correlate.4 = bf16[64,64,128]{2,1,0:T(8,128)(2,1)} custom-call(bf16[64,1,2,32,128]{4,3,2,1,0:T(8,128)(2,1)} %copy-done.6, bf16[64,1,2,32,128]{4,3,2,1,0:T(8,128)(2,1)} %all-to-all-done.1.refs_1_, bf16[256,256]{1,0:T(8,128)(2,1)S(1)} %copy-done.11, bf16[128,64,192]{2,1,0:T(8,128)(2,1)} %get-tuple-element.27.refs_3_.refs_2_, ...), custom_call_target="tpu_custom_call" | custom-call | flops 12000000000 | bytes 41943040 | tf_op jit(solution)/shard_map/cond/branch_0_fun/correlate/pallas_call | solution.py:252
  95.6 21.9 %all-to-all-done.3.refs_0_ = bf16[64,2,2,32,128]{4,3,2,1,0:T(8,128)(2,1)S(1)} async-done(((bf16[64,2,2,32,128]{4,3,2,1,0:T(8,128)(2,1)}), bf16[64,2,2,32,128]{4,3,2,1,0:T(8,128)(2,1)S(1)}, u32[]{:S(2)}, u32[]{:S(2)}) %all-to-all-start.3) | async-done | bytes 2097184 | tf_op jit(solution)/shard_map/cond/branch_0_fun/all_to_all | solution.py:363
  117.5 6.9 %all-to-all-start.2 = ((bf16[64,64,128]{2,1,0:T(8,128)(2,1)}), bf16[64,64,128]{2,1,0:T(8,128)(2,1)}, u32[]{:S(2)}, u32[]{:S(2)}) async-start(bf16[64,64,128]{2,1,0:T(8,128)(2,1)} %correlate.4), calls=%async_computation.2 | async-start | bytes 2097152 | tf_op jit(solution)/shard_map/cond/branch_0_fun/all_to_all | solution.py:363
  124.5 20.8 %correlate.5 = bf16[64,64,128]{2,1,0:T(8,128)(2,1)} custom-call(bf16[64,2,2,32,128]{4,3,2,1,0:T(8,128)(2,1)} %copy-done.4, bf16[256,256]{1,0:T(8,128)(2,1)S(1)} %copy-done.11, bf16[128,64,192]{2,1,0:T(8,128)(2,1)} %get-tuple-element.27.refs_3_.refs_2_, bf16[128,64,192]{2,1,0:T(8,128)(2,1)} %get-tuple-element.28.refs_4_.refs_3_, bf16[256,256]{1,0:T(8,128)(2,1)S(1)} %copy-done.9), custom_call_target="tpu_custom_call" | custom-call | flops 12000000000 | bytes 41943040 | tf_op jit(solution)/shard_map/cond/branch_0_fun/correlate/pallas_call | solution.py:252
  145.3 2.6 %all-to-all-done.2 = bf16[64,64,128]{2,1,0:T(8,128)(2,1)} async-done(((bf16[64,64,128]{2,1,0:T(8,128)(2,1)}), bf16[64,64,128]{2,1,0:T(8,128)(2,1)}, u32[]{:S(2)}, u32[]{:S(2)}) %all-to-all-start.2) | async-done | bytes 1048608 | tf_op jit(solution)/shard_map/cond/branch_0_fun/all_to_all | solution.py:363
  147.9 8.5 %all-to-all-start.7 = ((bf16[64,64,128]{2,1,0:T(8,128)(2,1)}), bf16[64,64,128]{2,1,0:T(8,128)(2,1)S(1)}, u32[]{:S(2)}, u32[]{:S(2)}) async-start(bf16[64,64,128]{2,1,0:T(8,128)(2,1)} %get-tuple-element.52), calls=%async_computation.7 | async-start | bytes 2097152 | tf_op jit(solution)/shard_map/all_to_all | solution.py:363
  158.4 2.4 %collective-permute-start.1 = (bf16[1,128,128]{2,1,0:T(8,128)(2,1)S(1)}, bf16[1,128,128]{2,1,0:T(8,128)(2,1)S(1)}, u32[]{:S(2)}, u32[]{:S(2)}) collective-permute-start(bf16[1,128,128]{2,1,0:T(8,128)(2,1)S(1)} %get-tuple-element.69), channel_id=1, source_target_pairs={{64,0},{128,64},{192,128},{65,1},{129,65},{193,129},{66,2},{130,66... | collective-permute-start | bytes 98312 | tf_op jit(solution)/shard_map/ppermute | solution.py:353
  160.9 3.2 %unpack.2.refs_2_ = bf16[1,32,2,64,128]{4,3,2,1,0:T(8,128)(2,1)S(1)} custom-call(bf16[64,64,128]{2,1,0:T(8,128)(2,1)} %get-tuple-element.50.in_ref), custom_call_target="tpu_custom_call" | custom-call | bytes 8388608 | tf_op jit(solution)/shard_map/unpack/pallas_call | solution.py:145
  166.4 4.1 %collective-permute-start.4 = (bf16[1,32,2,64,128]{4,3,2,1,0:T(8,128)(2,1)S(1)}, bf16[1,32,2,64,128]{4,3,2,1,0:T(8,128)(2,1)}, u32[]{:S(2)}, u32[]{:S(2)}) collective-permute-start(bf16[1,32,2,64,128]{4,3,2,1,0:T(8,128)(2,1)S(1)} %unpack.2.refs_2_), channel_id=1, source_target_pairs={{64,128},{128,64},{65,129},{129,65},{66,130},{130,66},{67,131},{13... | collective-permute-start | bytes 3145736 | tf_op jit(solution)/shard_map/ppermute | solution.py:359
  170.5 10.0 %all-to-all-done.7.in_ref = bf16[64,64,128]{2,1,0:T(8,128)(2,1)S(1)} async-done(((bf16[64,64,128]{2,1,0:T(8,128)(2,1)}), bf16[64,64,128]{2,1,0:T(8,128)(2,1)S(1)}, u32[]{:S(2)}, u32[]{:S(2)}) %all-to-all-start.7) | async-done | bytes 1048608 | tf_op jit(solution)/shard_map/all_to_all | solution.py:363
  182.6 4.9 %collective-permute-start.6 = (bf16[1,16,2,64,128]{4,3,2,1,0:T(8,128)(2,1)S(1)}, bf16[1,16,2,64,128]{4,3,2,1,0:T(8,128)(2,1)S(1)}, u32[]{:S(2)}, u32[]{:S(2)}) collective-permute-start(bf16[1,16,2,64,128]{4,3,2,1,0:T(8,128)(2,1)S(1)} %get-tuple-element.57), channel_id=1, source_target_pairs={{64,128},{128,64},{65,129},{129,65},{66,130},{130,66},{67,131},{13... | collective-permute-start | bytes 1572872 | tf_op jit(solution)/shard_map/ppermute | solution.py:359
  187.5 2.2 %collective-permute-start.5 = (bf16[1,16,2,64,128]{4,3,2,1,0:T(8,128)(2,1)S(1)}, bf16[1,16,2,64,128]{4,3,2,1,0:T(8,128)(2,1)}, u32[]{:S(2)}, u32[]{:S(2)}) collective-permute-start(bf16[1,16,2,64,128]{4,3,2,1,0:T(8,128)(2,1)S(1)} %get-tuple-element.54), channel_id=1, source_target_pairs={{64,128},{128,64},{65,129},{129,65},{66,130},{130,66},{67,131},{13... | collective-permute-start | bytes 1572872 | tf_op jit(solution)/shard_map/ppermute | solution.py:359
  189.7 4.9 %collective-permute-done.6.refs_5_ = bf16[1,16,2,64,128]{4,3,2,1,0:T(8,128)(2,1)S(1)} collective-permute-done((bf16[1,16,2,64,128]{4,3,2,1,0:T(8,128)(2,1)S(1)}, bf16[1,16,2,64,128]{4,3,2,1,0:T(8,128)(2,1)S(1)}, u32[]{:S(2)}, u32[]{:S(2)}) %collective-permute-start.6) | collective-permute-done | bytes 524320 | tf_op jit(solution)/shard_map/ppermute | solution.py:359
  195.4 4.9 %screen.2 = (bf16[1,32,4,128,128]{4,3,2,1,0:T(8,128)(2,1)}, bf16[1,32,2,128,128]{4,3,2,1,0:T(8,128)(2,1)}) custom-call(bf16[1,32,2,64,128]{4,3,2,1,0:T(8,128)(2,1)} %collective-permute-done.2.refs_0_, bf16[1,32,2,64,128]{4,3,2,1,0:T(8,128)(2,1)} %collective-permute-done.3.refs_1_, bf16[1,32,2,64,128]{4,3,2,1,0:T(8,128)(2,1)} %copy-done, ...), custom_call_target="tpu_custom_call" | custom-call | flops 2000000000 | bytes 10485760 | tf_op jit(solution)/shard_map/screen/pallas_call | solution.py:323
  200.4 5.0 %screen.3 = (bf16[1,32,4,128,128]{4,3,2,1,0:T(8,128)(2,1)}, bf16[1,32,2,128,128]{4,3,2,1,0:T(8,128)(2,1)}) custom-call(bf16[1,32,2,64,128]{4,3,2,1,0:T(8,128)(2,1)} %collective-permute-done.2.refs_0_, bf16[1,32,2,64,128]{4,3,2,1,0:T(8,128)(2,1)} %collective-permute-done.3.refs_1_, ...), custom_call_target="tpu_custom_call", output_to_operand_aliasing={{0}: (8, {}), {1}: (9, {})} | custom-call | flops 2000000000 | bytes 10485760 | tf_op jit(solution)/shard_map/screen/pallas_call | solution.py:323
  (35 shorter events, 7.3 us)
Async XLA Ops:
  4.0 36.0 %all-to-all-start = ((bf16[64,1,2,32,128]{4,3,2,1,0:T(8,128)(2,1)}), bf16[64,1,2,32,128]{4,3,2,1,0:T(8,128)(2,1)S(1)}, u32[]{:S(2)}, u32[]{:S(2)}) async-start(bf16[64,1,2,32,128]{4,3,2,1,0:T(8,128)(2,1)} %pack.5), calls=%async_computation | async-start | bytes 2097152 | tf_op jit(solution)/shard_map/cond/branch_0_fun/all_to_all | solution.py:363
  17.5 33.1 %copy-start.2 = (bf16[1,32,2,128,128]{4,3,2,1,0:T(8,128)(2,1)S(1)}, bf16[1,32,2,128,128]{4,3,2,1,0:T(8,128)(2,1)}, u32[]{:S(2)}) copy-start(bf16[1,32,2,128,128]{4,3,2,1,0:T(8,128)(2,1)} %get-tuple-element.24.refs_0_) | copy-start | bytes 6291460 | tf_op jit(solution)/shard_map/cond
  40.0 15.6 %copy-start.6 = (bf16[64,1,2,32,128]{4,3,2,1,0:T(8,128)(2,1)}, bf16[64,1,2,32,128]{4,3,2,1,0:T(8,128)(2,1)S(1)}, u32[]{:S(2)}) copy-start(bf16[64,1,2,32,128]{4,3,2,1,0:T(8,128)(2,1)S(1)} %all-to-all-done.refs_0_) | copy-start | bytes 3145732 | tf_op jit(solution)/shard_map/cond
  40.0 29.2 %all-to-all-start.1 = ((bf16[64,1,2,32,128]{4,3,2,1,0:T(8,128)(2,1)}), bf16[64,1,2,32,128]{4,3,2,1,0:T(8,128)(2,1)}, u32[]{:S(2)}, u32[]{:S(2)}) async-start(bf16[64,1,2,32,128]{4,3,2,1,0:T(8,128)(2,1)} %pack.6), calls=%async_computation.1 | async-start | bytes 2097152 | tf_op jit(solution)/shard_map/cond/branch_0_fun/all_to_all | solution.py:363
  55.6 19.2 %copy-start.9 = (bf16[256,256]{1,0:T(8,128)(2,1)S(1)}, bf16[256,256]{1,0:T(8,128)(2,1)}, u32[]{:S(2)}) copy-start(bf16[256,256]{1,0:T(8,128)(2,1)} %get-tuple-element.29.refs_5_.refs_4_) | copy-start | bytes 393220 | tf_op jit(solution)/shard_map/cond
  55.6 19.2 %copy-start.11 = (bf16[256,256]{1,0:T(8,128)(2,1)S(1)}, bf16[256,256]{1,0:T(8,128)(2,1)}, u32[]{:S(2)}) copy-start(bf16[256,256]{1,0:T(8,128)(2,1)} %get-tuple-element.26.refs_2_.refs_1_) | copy-start | bytes 393220 | tf_op jit(solution)/shard_map/cond
  69.2 48.4 %all-to-all-start.3 = ((bf16[64,2,2,32,128]{4,3,2,1,0:T(8,128)(2,1)}), bf16[64,2,2,32,128]{4,3,2,1,0:T(8,128)(2,1)S(1)}, u32[]{:S(2)}, u32[]{:S(2)}) async-start(bf16[64,2,2,32,128]{4,3,2,1,0:T(8,128)(2,1)} %pack.7), calls=%async_computation.3 | async-start | bytes 4194304 | tf_op jit(solution)/shard_map/cond/branch_0_fun/all_to_all | solution.py:363
  117.5 6.9 %copy-start.4 = (bf16[64,2,2,32,128]{4,3,2,1,0:T(8,128)(2,1)}, bf16[64,2,2,32,128]{4,3,2,1,0:T(8,128)(2,1)S(1)}, u32[]{:S(2)}) copy-start(bf16[64,2,2,32,128]{4,3,2,1,0:T(8,128)(2,1)S(1)} %all-to-all-done.3.refs_0_) | copy-start | bytes 6291460 | tf_op jit(solution)/shard_map/cond
  117.5 30.3 %all-to-all-start.2 = ((bf16[64,64,128]{2,1,0:T(8,128)(2,1)}), bf16[64,64,128]{2,1,0:T(8,128)(2,1)}, u32[]{:S(2)}, u32[]{:S(2)}) async-start(bf16[64,64,128]{2,1,0:T(8,128)(2,1)} %correlate.4), calls=%async_computation.2 | async-start | bytes 2097152 | tf_op jit(solution)/shard_map/cond/branch_0_fun/all_to_all | solution.py:363
  147.9 8.5 %copy-start.7 = (bf16[1,2,128,128]{3,2,1,0:T(8,128)(2,1)S(1)}, bf16[1,2,128,128]{3,2,1,0:T(8,128)(2,1)}, u32[]{:S(2)}) copy-start(bf16[1,2,128,128]{3,2,1,0:T(8,128)(2,1)} %param.11) | copy-start | bytes 196612
  147.9 32.6 %all-to-all-start.7 = ((bf16[64,64,128]{2,1,0:T(8,128)(2,1)}), bf16[64,64,128]{2,1,0:T(8,128)(2,1)S(1)}, u32[]{:S(2)}, u32[]{:S(2)}) async-start(bf16[64,64,128]{2,1,0:T(8,128)(2,1)} %get-tuple-element.52), calls=%async_computation.7 | async-start | bytes 2097152 | tf_op jit(solution)/shard_map/all_to_all | solution.py:363
  156.4 7.7 %collective-permute-start = (bf16[1,128,128]{2,1,0:T(8,128)(2,1)S(1)}, bf16[1,128,128]{2,1,0:T(8,128)(2,1)S(1)}, u32[]{:S(2)}, u32[]{:S(2)}) collective-permute-start(bf16[1,128,128]{2,1,0:T(8,128)(2,1)S(1)} %get-tuple-element.70), channel_id=1, source_target_pairs={{0,64},{64,128},{128,192},{1,65},{65,129},{129,193},{2,66},{66,130... | collective-permute-start | bytes 98312 | tf_op jit(solution)/shard_map/ppermute | solution.py:348
  158.4 7.3 %collective-permute-start.1 = (bf16[1,128,128]{2,1,0:T(8,128)(2,1)S(1)}, bf16[1,128,128]{2,1,0:T(8,128)(2,1)S(1)}, u32[]{:S(2)}, u32[]{:S(2)}) collective-permute-start(bf16[1,128,128]{2,1,0:T(8,128)(2,1)S(1)} %get-tuple-element.69), channel_id=1, source_target_pairs={{64,0},{128,64},{192,128},{65,1},{129,65},{193,129},{66,2},{130,66... | collective-permute-start | bytes 98312 | tf_op jit(solution)/shard_map/ppermute | solution.py:353
  164.1 6.3 %copy-start = (bf16[1,32,2,64,128]{4,3,2,1,0:T(8,128)(2,1)}, bf16[1,32,2,64,128]{4,3,2,1,0:T(8,128)(2,1)S(1)}, u32[]{:S(2)}) copy-start(bf16[1,32,2,64,128]{4,3,2,1,0:T(8,128)(2,1)S(1)} %unpack.2.refs_2_) | copy-start | bytes 3145732
  166.4 23.3 %collective-permute-start.4 = (bf16[1,32,2,64,128]{4,3,2,1,0:T(8,128)(2,1)S(1)}, bf16[1,32,2,64,128]{4,3,2,1,0:T(8,128)(2,1)}, u32[]{:S(2)}, u32[]{:S(2)}) collective-permute-start(bf16[1,32,2,64,128]{4,3,2,1,0:T(8,128)(2,1)S(1)} %unpack.2.refs_2_), channel_id=1, source_target_pairs={{64,128},{128,64},{65,129},{129,65},{66,130},{130,66},{67,131},{13... | collective-permute-start | bytes 3145736 | tf_op jit(solution)/shard_map/ppermute | solution.py:359
  170.4 19.3 %collective-permute-start.2 = (bf16[1,32,2,64,128]{4,3,2,1,0:T(8,128)(2,1)S(1)}, bf16[1,32,2,64,128]{4,3,2,1,0:T(8,128)(2,1)}, u32[]{:S(2)}, u32[]{:S(2)}) collective-permute-start(bf16[1,32,2,64,128]{4,3,2,1,0:T(8,128)(2,1)S(1)} %unpack.2.refs_2_), channel_id=1, source_target_pairs={{0,64},{128,192},{64,0},{192,128},{1,65},{129,193},{65,1},{193,129... | collective-permute-start | bytes 3145736 | tf_op jit(solution)/shard_map/ppermute | solution.py:359
  182.5 7.2 %copy-start.1 = (bf16[1,32,2,64,128]{4,3,2,1,0:T(8,128)(2,1)}, bf16[1,32,2,64,128]{4,3,2,1,0:T(8,128)(2,1)S(1)}, u32[]{:S(2)}) copy-start(bf16[1,32,2,64,128]{4,3,2,1,0:T(8,128)(2,1)S(1)} %get-tuple-element.53.refs_3_) | copy-start | bytes 3145732
  182.5 12.9 %collective-permute-start.3 = (bf16[1,32,2,64,128]{4,3,2,1,0:T(8,128)(2,1)S(1)}, bf16[1,32,2,64,128]{4,3,2,1,0:T(8,128)(2,1)}, u32[]{:S(2)}, u32[]{:S(2)}) collective-permute-start(bf16[1,32,2,64,128]{4,3,2,1,0:T(8,128)(2,1)S(1)} %get-tuple-element.53.refs_3_), channel_id=1, source_target_pairs={{0,64},{128,192},{64,0},{192,128},{1,65},{129,193},{65,1},{193,129... | collective-permute-start | bytes 3145736 | tf_op jit(solution)/shard_map/ppermute | solution.py:359
  182.6 12.0 %collective-permute-start.6 = (bf16[1,16,2,64,128]{4,3,2,1,0:T(8,128)(2,1)S(1)}, bf16[1,16,2,64,128]{4,3,2,1,0:T(8,128)(2,1)S(1)}, u32[]{:S(2)}, u32[]{:S(2)}) collective-permute-start(bf16[1,16,2,64,128]{4,3,2,1,0:T(8,128)(2,1)S(1)} %get-tuple-element.57), channel_id=1, source_target_pairs={{64,128},{128,64},{65,129},{129,65},{66,130},{130,66},{67,131},{13... | collective-permute-start | bytes 1572872 | tf_op jit(solution)/shard_map/ppermute | solution.py:359
  187.5 12.9 %collective-permute-start.5 = (bf16[1,16,2,64,128]{4,3,2,1,0:T(8,128)(2,1)S(1)}, bf16[1,16,2,64,128]{4,3,2,1,0:T(8,128)(2,1)}, u32[]{:S(2)}, u32[]{:S(2)}) collective-permute-start(bf16[1,16,2,64,128]{4,3,2,1,0:T(8,128)(2,1)S(1)} %get-tuple-element.54), channel_id=1, source_target_pairs={{64,128},{128,64},{65,129},{129,65},{66,130},{130,66},{67,131},{13... | collective-permute-start | bytes 1572872 | tf_op jit(solution)/shard_map/ppermute | solution.py:359
  194.6 0.8 copy-start.8
